TPU v7x, 32 devices: a whole 2x2x4 slice. The times are simulated.
32 devices in a mesh: dates: 2 (over y), az: 16 (over z, x, core).
Axes of the slice: x: 2, y: 2, z: 4, core: 2. Of those that a mesh axis runs over, the one named last changes fastest.
Arguments:
- secondary_pieces: bfloat16 [4096, 2, 16, 256], P(('dates', 'az')), parts along dimension 0, may hold values from -6 to 6
- piece_target: int32 [4096, 1], P(('dates', 'az')), parts along dimension 0, may hold values from 0 to 15; in each aligned block of 128 rows (0 to 127, 128 to 255, ...) at most 16 rows name the same one
- piece_block: int32 [4096], P(('dates', 'az')), parts along dimension 0, may hold values from 0 to 63
- piece_row: int32 [4096], P(('dates', 'az')), parts along dimension 0, may hold values from 0 to 248
- piece_column: int32 [4096], P(('dates', 'az')), parts along dimension 0, may hold values from -4 to 4
- ramp_rate: float32 [32, 256], P(('dates', 'az')), parts along dimension 0, may hold values from 20 to 200
- centroid: float32 [32, 256], P(('dates', 'az')), parts along dimension 0, may hold values from -8 to 8
- sinc_blocks: float32 [64, 8, 8], replicated, may hold values from -0.75 to 0.75
- reference_tile: float32 [2, 8192, 256], P(None, ('dates', 'az')), parts along dimension 1, may hold values from -6 to 6
- intersection_rows: int32 [32], P(('dates', 'az')), parts along dimension 0, may hold values from 16 to 32, as said below
Outputs:
- coregistered: bfloat16 [4096, 2, 8, 256], P(('dates', 'az')), parts along dimension 0
- interferogram: float32 [2, 8192, 256], P(None, ('dates', 'az')), parts along dimension 1
- diversity_sum: float32 [32, 2, 256], P(('dates', 'az')), parts along dimension 0
There are 2 independent parts, one for each index of `dates`. A program takes and returns all parts, laid end to end along the dimension named above; an argument that names none is the same for every part. Nothing has to cross between parts.
Inputs may be any that keep to these rules, and one draw needn't show every extreme that they name: `piece_target`: of the 128 pieces of one device at most 16 land in the same tile, and in every draw some device sends exactly 16 to one tile. `intersection_rows`: some tile shares exactly 32 lines.
All inputs are finite; a program needn't handle non-finite values.
Results may differ from a plain program's by a relative error of at most 0.0076.
Values may be sent and summed in bfloat16 or wider, within the bound.
A program may use at most 128 MiB of HBM per device.

v0:
```python
import math

import jax
import jax.numpy as jnp
from jax import lax
from jax.sharding import PartitionSpec as P

TILE_ROWS = 256
INTERSECTION = 32
WEIGHT_BLOCKS = 64


def from_behind(value, axis, steps):
    count = lax.axis_size(axis)
    leading, last = (max(0, -steps), min(count, count - steps))
    return lax.ppermute(value, axis, [(source, source + steps) for source in range(leading, last)])


def ramp_phase(row_times, rate_table, centroid_table):
    scaled = ((row_times - 0.5 * TILE_ROWS) / TILE_ROWS)[:, :, None]
    return (
        jnp.pi * rate_table[:, None, :] * scaled * scaled
        + 2.0 * jnp.pi * centroid_table[:, None, :] * scaled
    )


def resample_group(
    pieces, block_index, row_start, col_shift, rate_table, centroid_table, sinc_blocks
):
    total = pieces.shape[0]
    width = pieces.shape[3]
    in_rows = pieces.shape[2]
    out_rows = in_rows - 8
    row_float = row_start.astype(jnp.float32)[:, None]
    phase_in = ramp_phase(
        row_float + jnp.arange(in_rows, dtype=jnp.float32)[None, :] - 3.0,
        rate_table,
        centroid_table,
    )
    cosine = jnp.cos(phase_in)
    sine_part = jnp.sin(phase_in)
    real_part = pieces[:, 0].astype(jnp.float32)
    imag_part = pieces[:, 1].astype(jnp.float32)
    deramped = jnp.stack(
        [real_part * cosine + imag_part * sine_part, imag_part * cosine - real_part * sine_part],
        axis=1,
    ).astype(jnp.bfloat16)
    table_size = sinc_blocks.shape[0]
    one_hot = (block_index[:, None] == jnp.arange(table_size)[None, :]).astype(jnp.float32)
    selected = jnp.dot(
        one_hot, sinc_blocks.reshape(table_size, 64), precision=lax.Precision.HIGHEST
    ).reshape(total, 8, 8)
    shifter = (
        jnp.arange(in_rows)[None, None, :]
        == jnp.arange(out_rows)[None, :, None] + jnp.arange(8)[:, None, None]
    ).astype(jnp.float32)
    band_taps = jnp.einsum(
        "nab,arq->nrbq", selected, shifter, precision=lax.Precision.HIGHEST
    ).astype(jnp.bfloat16)
    offsets = jnp.arange(16, dtype=jnp.int32)
    tap_of_offset = offsets[None, :] + 1 - col_shift[:, None] - 5
    offset_pick = tap_of_offset[:, :, None] == jnp.arange(8, dtype=jnp.int32)[None, None, :]
    band_offsets = jnp.sum(
        jnp.where(
            offset_pick[:, None, :, :, None],
            band_taps[:, :, None, :, :],
            jnp.zeros((), jnp.bfloat16),
        ),
        axis=3,
    )
    row_mixed = jnp.einsum(
        "nroq,nzqc->nzorc", band_offsets, deramped, preferred_element_type=jnp.float32
    )
    padded = jnp.pad(row_mixed, ((0, 0), (0, 0), (0, 0), (0, 0), (8, 8)))
    interpolated = padded[:, :, 0, :, 1 : 1 + width]
    for offset_number in range(1, 16):
        interpolated = (
            interpolated
            + padded[:, :, offset_number, :, offset_number + 1 : offset_number + 1 + width]
        )
    out_times = (
        row_float
        + jnp.arange(out_rows, dtype=jnp.float32)[None, :]
        + block_index.astype(jnp.float32)[:, None] / WEIGHT_BLOCKS
    )
    phase_out = ramp_phase(out_times, rate_table, centroid_table)
    cosine_out = jnp.cos(phase_out)
    sine_out = jnp.sin(phase_out)
    out_real = interpolated[:, 0] * cosine_out - interpolated[:, 1] * sine_out
    out_imag = interpolated[:, 1] * cosine_out + interpolated[:, 0] * sine_out
    return jnp.stack([out_real, out_imag], axis=1).astype(jnp.bfloat16)


def resample_all(
    pieces, block_index, row_start, col_shift, rate_table, centroid_table, sinc_blocks
):
    total = pieces.shape[0]
    group_size = math.gcd(total, 128)
    group_count = total // group_size

    def split_up(array_item):
        return array_item.reshape((group_count, group_size) + array_item.shape[1:])

    def one_group(bundle):
        return resample_group(
            bundle[0], bundle[1], bundle[2], bundle[3], bundle[4], bundle[5], sinc_blocks
        )

    bundles = tuple(
        (
            split_up(array_item)
            for array_item in (
                pieces,
                block_index,
                row_start,
                col_shift,
                rate_table,
                centroid_table,
            )
        )
    )
    result = lax.map(one_group, bundles)
    return result.reshape((total,) + result.shape[2:])


def on_device(
    secondary_pieces,
    piece_target,
    piece_block,
    piece_row,
    piece_column,
    ramp_rate,
    centroid,
    sinc_blocks,
    reference_tile,
    intersection_rows,
):
    piece_count = secondary_pieces.shape[0]
    tile_count = lax.axis_size("az")
    capacity = max(2, 2 * piece_count // tile_count)
    slot_total = tile_count * capacity
    width = secondary_pieces.shape[3]
    tile_rows = reference_tile.shape[1]
    out_rows = secondary_pieces.shape[2] - 8
    target = piece_target[:, 0]
    same_target = target[:, None] == target[None, :]
    earlier_piece = jnp.arange(piece_count)[:, None] > jnp.arange(piece_count)[None, :]
    rank_within = jnp.sum(same_target & earlier_piece, axis=1, dtype=jnp.int32)
    slot_index = target * capacity + rank_within
    present = jnp.ones((piece_count,), jnp.int32)
    send_data = (
        jnp.zeros((slot_total,) + secondary_pieces.shape[1:], jnp.bfloat16)
        .at[slot_index]
        .set(secondary_pieces)
    )
    send_info = (
        jnp.zeros((slot_total, 4), jnp.int32)
        .at[slot_index]
        .set(jnp.stack([present, piece_block, piece_row, piece_column], axis=1))
    )
    got_data, got_info = (
        lax.all_to_all(send_data, "az", split_axis=0, concat_axis=0, tiled=True),
        lax.all_to_all(send_info, "az", split_axis=0, concat_axis=0, tiled=True),
    )
    rate_rows = jnp.broadcast_to(ramp_rate, (slot_total, width))
    centroid_rows = jnp.broadcast_to(centroid, (slot_total, width))
    resampled = resample_all(
        got_data,
        got_info[:, 1],
        got_info[:, 2],
        got_info[:, 3],
        rate_rows,
        centroid_rows,
        sinc_blocks,
    )
    returned = lax.all_to_all(resampled, "az", split_axis=0, concat_axis=0, tiled=True)
    coregistered = returned[slot_index]
    valid_slot = got_info[:, 0]
    row_start = got_info[:, 2]
    placement = (
        row_start[None, :, None] + jnp.arange(out_rows)[None, None, :]
        == jnp.arange(tile_rows)[:, None, None]
    )
    placement = (placement & (valid_slot[None, :, None] == 1)).astype(jnp.bfloat16)
    assembled = jnp.einsum(
        "tsr,szrc->ztc", placement, resampled, preferred_element_type=jnp.float32
    )
    inter_real = reference_tile[0] * assembled[0] + reference_tile[1] * assembled[1]
    inter_imag = reference_tile[1] * assembled[0] - reference_tile[0] * assembled[1]
    interferogram = jnp.stack([inter_real, inter_imag], axis=0)
    tail_rows = interferogram[:, tile_rows - INTERSECTION :, :]
    previous = from_behind(tail_rows, "az", 1)
    intersection_len = intersection_rows[0]
    positions = jnp.arange(INTERSECTION, dtype=jnp.int32)
    aligned = jnp.take(
        previous, (positions + INTERSECTION - intersection_len) % INTERSECTION, axis=1
    )
    head_rows = interferogram[:, :INTERSECTION, :]
    row_mask = (positions < intersection_len).astype(jnp.float32)[:, None]
    product_real = jnp.sum(
        (head_rows[0] * aligned[0] + head_rows[1] * aligned[1]) * row_mask, axis=0
    )
    product_imag = jnp.sum(
        (head_rows[1] * aligned[0] - head_rows[0] * aligned[1]) * row_mask, axis=0
    )
    length_float = intersection_len.astype(jnp.float32)
    diversity = jnp.stack([product_real / length_float, product_imag / length_float], axis=0)
    return (coregistered, interferogram, diversity[None])


def solution(mesh):
    return jax.shard_map(
        on_device,
        mesh=mesh,
        in_specs=(
            P(("dates", "az"), None, None, None),
            P(("dates", "az"), None),
            P(("dates", "az")),
            P(("dates", "az")),
            P(("dates", "az")),
            P(("dates", "az"), None),
            P(("dates", "az"), None),
            P(),
            P(None, ("dates", "az"), None),
            P(("dates", "az")),
        ),
        out_specs=(
            P(("dates", "az"), None, None, None),
            P(None, ("dates", "az"), None),
            P(("dates", "az"), None, None),
        ),
        check_vma=False,
    )
```

profile of v0, /device:TPU:12, one launch (start us, length us, event | category | flops | bytes accessed | tf_op | source)
XLA Modules:
  0.0 469.3 jit_solution(5545171470380177666)
XLA Ops:
  1.5 0.9 convert_reduce_fusion
  3.1 0.9 scatter_custom_fusion.1
  4.8 6.3 %all-to-all-start.1 = ((s32[16,16,4]{1,2,0:T(4,128)}), s32[16,16,4]{1,2,0:T(4,128)S(1)}, u32[]{:S(2)}, u32[]{:S(2)}) async-start(s32[16,16,4]{1,2,0:T(4,128)} %copy.84), calls=%async_computation.1 | async-start | bytes 65536 | tf_op jit(solution)/shard_map/all_to_all | solution.py:163
  11.1 2.5 broadcast_in_dim.106
  13.5 15.7 %scatter_fusion = bf16[256,2,16,256]{3,2,1,0:T(8,128)(2,1)} fusion(bf16[256,2,16,256]{3,2,1,0:T(8,128)(2,1)} %broadcast_in_dim.106, s32[128]{0:T(128)S(1)} %fusion.61, bf16[128,2,16,256]{3,2,1,0:T(8,128)(2,1)S(1)} %copy-done), kind=kCustom, calls=%fused_computation.2 | custom fusion | bytes 6291968 | tf_op jit(solution)/shard_map/scatter | solution.py:154
  29.3 6.1 %all-to-all-start = ((bf16[256,2,16,256]{3,2,1,0:T(8,128)(2,1)}), bf16[256,2,16,256]{3,2,1,0:T(8,128)(2,1)}, u32[]{:S(2)}, u32[]{:S(2)}) async-start(bf16[256,2,16,256]{3,2,1,0:T(8,128)(2,1)} %scatter_fusion), calls=%async_computation | async-start | bytes 8388608 | tf_op jit(solution)/shard_map/all_to_all | solution.py:162
  35.5 90.7 %all-to-all-done = bf16[256,2,16,256]{3,2,1,0:T(8,128)(2,1)} async-done(((bf16[256,2,16,256]{3,2,1,0:T(8,128)(2,1)}), bf16[256,2,16,256]{3,2,1,0:T(8,128)(2,1)}, u32[]{:S(2)}, u32[]{:S(2)}) %all-to-all-start) | async-done | bytes 4194336 | tf_op jit(solution)/shard_map/all_to_all | solution.py:162
  126.3 288.8 %while.15 = (s32[]{:T(128)}, bf16[2,128,2,8,256]{4,3,2,1,0:T(8,128)(2,1)}, bf16[2,128,2,16,256]{4,3,2,1,0:T(8,128)(2,1)}, f32[2,128,256]{2,1,0:T(8,128)S(1)}, s3...) while((s32[]{:T(128)}, ...), condition=%wide.region_5.6_spmd, body=%wide.region_3.5_spmd.sunk | while | flops 314547648 | bytes 97447160 | solution.py:122
  126.5 1.8 dynamic-slice_bitcast_fusion.2
  128.2 9.0 %fusion.86 = (bf16[128,1,16,256]{3,2,1,0:T(8,128)(2,1)S(1)}, bf16[128,1,16,256]{3,2,1,0:T(8,128)(2,1)S(1)}) fusion(f32[128,256]{1,0:T(8,128)S(1)} %get-tuple-element.319, f32[128,16]{1,0:T(8,128)S(1)} %copy.119, f32[128,256]{1,0:T(8,128)S(1)} %get-tuple-element.321, bf16[128,2,16,256]{3,2,1,0:T(8,128)(2,1)S(1)} %dynamic-slice_bitcast_fusion.2), kind=kLoop, calls=%fused_computation.41.clone.1 | loop fusion | flops 6815744 | bytes 4464640 | tf_op jit(solution)/shard_map/convert.7
  138.0 1.1 select_reduce_fusion.2
  139.2 6.4 %copy.118 = bf16[128,8,16,16,1]{3,2,1,4,0:T(8,128)(2,1)} copy(bf16[128,8,16,16,1]{0,3,2,1,4:T(8,128)(2,1)S(1)} %bitcast.177) | data formatting | bytes 1048576 | tf_op jit(solution)/shard_map/while/body/eval_jaxpr/reduce_sum | solution.py:63
  145.6 15.4 %convolution_bitcast_fusion.5 = f32[128,2,16,8,256]{4,2,3,1,0:T(8,128)} fusion(bf16[128,8,16,16,1]{3,2,1,4,0:T(8,128)(2,1)} %copy.118, bf16[128,1,16,256]{3,2,1,0:T(8,128)(2,1)S(1)} %get-tuple-element.322, bf16[128,1,16,256]{3,2,1,0:T(8,128)(2,1)S(1)} %get-tuple-element.323), kind=kOutput, calls=%fused_computation.19.clone.1 | convolution fusion | flops 272629760 | bytes 36175872 | tf_op jit(solution)/shard_map/while/body/eval_jaxpr/nroq,nzqc->nzorc/dot_general | solution.py:71
  161.0 99.1 %fusion.87 = f32[128,2,1,8,256]{4,2,3,1,0:T(1,128)S(1)} fusion(f32[128,2,16,8,256]{4,2,3,1,0:T(8,128)} %convolution_bitcast_fusion.5), kind=kLoop, calls=%fused_computation.38.clone.1 | loop fusion | flops 7864320 | bytes 37748736 | tf_op jit(solution)/shard_map/while/body/eval_jaxpr/add | solution.py:78
  260.4 4.6 fusion.89
  265.0 4.6 fusion.88
  269.6 1.0 copy_dynamic-update-slice_fusion.2
  270.8 1.8 dynamic-slice_bitcast_fusion.2
  272.6 9.0 %fusion.86 = (bf16[128,1,16,256]{3,2,1,0:T(8,128)(2,1)S(1)}, bf16[128,1,16,256]{3,2,1,0:T(8,128)(2,1)S(1)}) fusion(f32[128,256]{1,0:T(8,128)S(1)} %get-tuple-element.319, f32[128,16]{1,0:T(8,128)S(1)} %copy.119, f32[128,256]{1,0:T(8,128)S(1)} %get-tuple-element.321, bf16[128,2,16,256]{3,2,1,0:T(8,128)(2,1)S(1)} %dynamic-slice_bitcast_fusion.2), kind=kLoop, calls=%fused_computation.41.clone.1 | loop fusion | flops 6815744 | bytes 4464640 | tf_op jit(solution)/shard_map/convert.7
  282.4 1.1 select_reduce_fusion.2
  283.5 6.4 %copy.118 = bf16[128,8,16,16,1]{3,2,1,4,0:T(8,128)(2,1)} copy(bf16[128,8,16,16,1]{0,3,2,1,4:T(8,128)(2,1)S(1)} %bitcast.177) | data formatting | bytes 1048576 | tf_op jit(solution)/shard_map/while/body/eval_jaxpr/reduce_sum | solution.py:63
  290.0 15.4 %convolution_bitcast_fusion.5 = f32[128,2,16,8,256]{4,2,3,1,0:T(8,128)} fusion(bf16[128,8,16,16,1]{3,2,1,4,0:T(8,128)(2,1)} %copy.118, bf16[128,1,16,256]{3,2,1,0:T(8,128)(2,1)S(1)} %get-tuple-element.322, bf16[128,1,16,256]{3,2,1,0:T(8,128)(2,1)S(1)} %get-tuple-element.323), kind=kOutput, calls=%fused_computation.19.clone.1 | convolution fusion | flops 272629760 | bytes 36175872 | tf_op jit(solution)/shard_map/while/body/eval_jaxpr/nroq,nzqc->nzorc/dot_general | solution.py:71
  305.3 99.1 %fusion.87 = f32[128,2,1,8,256]{4,2,3,1,0:T(1,128)S(1)} fusion(f32[128,2,16,8,256]{4,2,3,1,0:T(8,128)} %convolution_bitcast_fusion.5), kind=kLoop, calls=%fused_computation.38.clone.1 | loop fusion | flops 7864320 | bytes 37748736 | tf_op jit(solution)/shard_map/while/body/eval_jaxpr/add | solution.py:78
  404.7 4.6 fusion.89
  409.4 4.6 fusion.88
  414.0 1.1 copy_dynamic-update-slice_fusion.2
  415.1 6.7 %all-to-all-start.2 = ((bf16[256,2,8,256]{3,2,1,0:T(8,128)(2,1)}), bf16[256,2,8,256]{3,2,1,0:T(8,128)(2,1)S(1)}, u32[]{:S(2)}, u32[]{:S(2)}) async-start(bf16[256,2,8,256]{3,2,1,0:T(8,128)(2,1)} %bitcast.36), calls=%async_computation.2 | async-start | bytes 4194304 | tf_op jit(solution)/shard_map/all_to_all | solution.py:176
  422.7 3.0 fusion.47
  425.8 2.1 collective-permute-start
  428.7 30.7 %collective-permute-done = f32[2,32,256]{2,1,0:T(8,128)S(1)} collective-permute-done((f32[2,32,256]{2,1,0:T(8,128)S(1)}, f32[2,32,256]{2,1,0:T(8,128)S(1)}, u32[]{:S(2)}, u32[]{:S(2)}) %collective-permute-start) | collective-permute-done | bytes 65568 | tf_op jit(solution)/shard_map/ppermute | solution.py:16
  460.8 6.9 %all-to-all-done.2 = bf16[256,2,8,256]{3,2,1,0:T(8,128)(2,1)S(1)} async-done(((bf16[256,2,8,256]{3,2,1,0:T(8,128)(2,1)}), bf16[256,2,8,256]{3,2,1,0:T(8,128)(2,1)S(1)}, u32[]{:S(2)}, u32[]{:S(2)}) %all-to-all-start.2) | async-done | bytes 2097184 | tf_op jit(solution)/shard_map/all_to_all | solution.py:176
  467.7 1.6 gather_fusion
  (70 shorter events, 7.4 us)
Async XLA Ops:
  3.1 10.4 %copy-start.3 = (s32[128]{0:T(128)}, s32[128]{0:T(128)S(1)}, u32[]{:S(2)}) copy-start(s32[128]{0:T(128)S(1)} %fusion.61) | copy-start | bytes 1540
  4.8 24.5 %all-to-all-start.1 = ((s32[16,16,4]{1,2,0:T(4,128)}), s32[16,16,4]{1,2,0:T(4,128)S(1)}, u32[]{:S(2)}, u32[]{:S(2)}) async-start(s32[16,16,4]{1,2,0:T(4,128)} %copy.84), calls=%async_computation.1 | async-start | bytes 65536 | tf_op jit(solution)/shard_map/all_to_all | solution.py:163
  11.1 2.5 copy-start
  29.2 97.0 %copy-start.5 = (f32[1,256]{1,0:T(1,128)S(1)}, f32[1,256]{1,0:T(1,128)}, u32[]{:S(2)}) copy-start(f32[1,256]{1,0:T(1,128)} %param.17) | copy-start | bytes 3076
  29.2 97.0 %copy-start.6 = (f32[1,256]{1,0:T(1,128)S(1)}, f32[1,256]{1,0:T(1,128)}, u32[]{:S(2)}) copy-start(f32[1,256]{1,0:T(1,128)} %param.18) | copy-start | bytes 3076
  29.3 97.0 %copy-start.1 = (f32[64,8,8]{0,2,1:T(8,128)S(1)}, f32[64,8,8]{0,2,1:T(8,128)}, u32[]{:S(2)}) copy-start(f32[64,8,8]{0,2,1:T(8,128)} %param.19) | copy-start | bytes 49156
  29.3 96.9 %all-to-all-start = ((bf16[256,2,16,256]{3,2,1,0:T(8,128)(2,1)}), bf16[256,2,16,256]{3,2,1,0:T(8,128)(2,1)}, u32[]{:S(2)}, u32[]{:S(2)}) async-start(bf16[256,2,16,256]{3,2,1,0:T(8,128)(2,1)} %scatter_fusion), calls=%async_computation | async-start | bytes 8388608 | tf_op jit(solution)/shard_map/all_to_all | solution.py:162
  415.1 7.4 %copy-start.4 = (s32[128]{0:T(128)S(1)}, s32[128]{0:T(128)}, u32[]{:S(2)}) copy-start(s32[128]{0:T(128)} %copy-done.3) | copy-start | bytes 1540
  415.1 52.6 %all-to-all-start.2 = ((bf16[256,2,8,256]{3,2,1,0:T(8,128)(2,1)}), bf16[256,2,8,256]{3,2,1,0:T(8,128)(2,1)S(1)}, u32[]{:S(2)}, u32[]{:S(2)}) async-start(bf16[256,2,8,256]{3,2,1,0:T(8,128)(2,1)} %bitcast.36), calls=%async_computation.2 | async-start | bytes 4194304 | tf_op jit(solution)/shard_map/all_to_all | solution.py:176
  422.7 3.0 copy-start.2
  425.8 33.6 %collective-permute-start = (f32[2,32,256]{2,1,0:T(8,128)S(1)}, f32[2,32,256]{2,1,0:T(8,128)S(1)}, u32[]{:S(2)}, u32[]{:S(2)}) collective-permute-start(f32[2,32,256]{2,1,0:T(8,128)S(1)} %fusion.52), channel_id=1, source_target_pairs={{0,1},{1,2},{2,3},{3,4},{4,5},{5,6},{6,7},{7,8},{8,9},{9,10},{10,1... | collective-permute-start | bytes 196616 | tf_op jit(solution)/shard_map/ppermute | solution.py:16
where the time goes:
time: 474 us; the launch traced here: 469 us
  other arithmetic  244 us (51%)
  waiting for transfers between devices  128 us (27%)
  local copies, waits for them, and re-layouts  39.6 us (8%)
  matrix products  35 us (7%)
  starting transfers between devices  21.1 us (4%)
    add x2, other arithmetic, resample_group(): interpolated + padded[:, :, offset_number, :, offset_number + 1:offset_nu...  198 us
    all_to_all x1, waiting for transfers between devices, on_device(): lax.all_to_all(send_data, 'az', split_axis=0, concat_axis=0, tiled=True)  90.7 us
    dot_general x2, matrix products, resample_group(): jnp.einsum('nroq,nzqc->nzorc', band_offsets, deramped, preferred_element_...  30.8 us
    ppermute x1, waiting for transfers between devices, from_behind(): lax.ppermute(value, axis, [(source, source + steps) for source in range(l...  30.7 us
    another operation x4, other arithmetic, resample_group(): return jnp.stack([out_real, out_imag], axis=1).astype(jnp.bfloat16)  18.4 us
    another operation x2, other arithmetic  18 us
    scatter x1, local copies, waits for them, and re-layouts, on_device(): send_data = jnp.zeros((slot_total,) + secondary_pieces.shape[1:], jnp.bfl...  15.7 us
    reduce_sum x2, local copies, waits for them, and re-layouts, resample_group(): jnp.sum(jnp.where(offset_pick[:, None, :, :, None], band_taps[:, :, None,...  12.9 us
  transfers between devices with their start and end apart: 4, of which 3 were waited for; matrix products, arithmetic and copies ran while one was open for 5% of the time, Pallas kernels for 0%

commit v1 on v0

v1 whole, which is shorter than its diff:
```python
import functools

import jax
import jax.numpy as jnp
from jax import lax
from jax.experimental import pallas as pl
from jax.experimental.pallas import tpu as pltpu
from jax.sharding import PartitionSpec as P

TILE_ROWS = 256
INTERSECTION = 32
WEIGHT_BLOCKS = 64
GROUP = 16
MESH = pl.DeviceIdType.MESH

SIN_FIT = (6.2831807136535645, -41.33925247192383, 81.40833282470703, -71.61119079589844)
COS_FIT = (0.9999932646751404, -19.73573875427246, 64.65997314453125, -78.21002960205078)


def unit_phasor(turns):
    part = turns - jnp.round(turns)
    w = 0.25 - jnp.abs(part)
    w2 = w * w
    even = jnp.full_like(w2, COS_FIT[-1])
    for coeff in COS_FIT[-2::-1]:
        even = even * w2 + coeff
    odd = jnp.full_like(w2, SIN_FIT[-1])
    for coeff in SIN_FIT[-2::-1]:
        odd = odd * w2 + coeff
    return odd * w, jnp.where(part < 0, -even, even)


def resample_kernel(
    capacity,
    target,
    block,
    row,
    col,
    x_ref,
    table_ref,
    taps_ref,
    out_ref,
    message_ref,
    lines_ref,
    deramped,
    band,
    mixed,
    used,
):
    step = pl.program_id(0)
    width = x_ref.shape[3]
    half = width // 2

    @pl.when(step == 0)
    def _():
        message_ref[...] = jnp.zeros_like(message_ref)
        lines_ref[...] = jnp.full_like(lines_ref, -1)

        @pl.loop(0, used.shape[0])
        def _(tile):
            used[tile] = 0

    in_iota = lax.broadcasted_iota(jnp.int32, (16, width), 0).astype(jnp.float32)
    out_iota = lax.broadcasted_iota(jnp.int32, (8, width), 0).astype(jnp.float32)
    band_lane = lax.broadcasted_iota(jnp.int32, (64, GROUP * 16), 1) // 16
    lane = lax.broadcasted_iota(jnp.int32, (8, half), 1)
    slot_lane = lax.broadcasted_iota(jnp.int32, (1, lines_ref.shape[2]), 1)
    slot_line = (slot_lane % 16) // 8 * TILE_ROWS + slot_lane % 8

    def table_rows(tile):
        return 0.5 * table_ref[tile, 0:1, :], table_ref[tile, 1:2, :]

    def before(i, _):
        p = step * GROUP + i
        rate, centre = table_rows(target[p])
        u = (in_iota + (row[p].astype(jnp.float32) - (3.0 + TILE_ROWS / 2))) * (1.0 / TILE_ROWS)
        cosine, sine = unit_phasor((rate * u + centre) * u)
        real = x_ref[i, 0].astype(jnp.float32)
        imag = x_ref[i, 1].astype(jnp.float32)
        lines = pl.ds(pl.multiple_of(i * 16, 16), 16)
        deramped[lines, 0:width] = (real * cosine + imag * sine).astype(jnp.bfloat16)
        deramped[lines, width : 2 * width] = (imag * cosine - real * sine).astype(jnp.bfloat16)
        taps = taps_ref[block[p]]
        band[pl.ds(pl.multiple_of(i * 64, 64), 64), :] = jnp.where(
            band_lane == i, taps, jnp.zeros_like(taps)
        )
        return 0

    lax.fori_loop(0, GROUP, before, 0, unroll=4)
    mixed[...] = jnp.dot(band[...], deramped[...], preferred_element_type=jnp.float32)

    def after(i, _):
        p = step * GROUP + i
        tile = target[p]
        shift0 = col[p] - 3
        sums = [jnp.zeros((8, half), jnp.float32) for _ in range(4)]
        for b in range(8):
            shift = shift0 + b
            turn = lax.rem(half - shift, half)
            place = lane + shift
            inside = (place >= 0) & (place < half)
            above = (shift > 0).astype(jnp.float32)
            below = (shift < 0).astype(jnp.float32)
            lines = pl.ds(pl.multiple_of(i * 64 + b * 8, 8), 8)
            for z in range(2):
                left = pltpu.roll(mixed[lines, z * width : z * width + half], turn, 1)
                right = pltpu.roll(mixed[lines, z * width + half : (z + 1) * width], turn, 1)
                sums[2 * z] = sums[2 * z] + jnp.where(inside, left, right * above)
                sums[2 * z + 1] = sums[2 * z + 1] + jnp.where(inside, right, left * below)
        real = jnp.concatenate(sums[0:2], axis=1)
        imag = jnp.concatenate(sums[2:4], axis=1)
        rate, centre = table_rows(tile)
        start = (
            row[p].astype(jnp.float32)
            + block[p].astype(jnp.float32) * (1.0 / WEIGHT_BLOCKS)
            - TILE_ROWS / 2
        )
        u = (out_iota + start) * (1.0 / TILE_ROWS)
        cosine, sine = unit_phasor((rate * u + centre) * u)
        out_real = real * cosine - imag * sine
        out_imag = imag * cosine + real * sine
        out_ref[i, 0] = out_real.astype(jnp.bfloat16)
        out_ref[i, 1] = out_imag.astype(jnp.bfloat16)
        slot = used[tile]
        used[tile] = slot + 1
        message_ref[tile, pl.ds(pl.multiple_of(slot * 16, 16), 16), :] = jnp.concatenate(
            [out_real, out_imag], axis=0
        ).astype(jnp.bfloat16)
        lines_ref[tile, 0:1, :] = jnp.where(
            slot_lane // 16 == slot, slot_line + row[p], lines_ref[tile, 0:1, :]
        )
        return 0

    lax.fori_loop(0, GROUP, after, 0, unroll=2)


def resample(pieces, target, block, row, col, tables, taps, capacity):
    count, _, in_rows, width = pieces.shape
    tiles = tables.shape[0]
    rows = capacity * 16
    lanes = max(128, rows)
    whole = lambda *shape: pl.BlockSpec(shape, lambda g, *_: (0,) * len(shape))
    return pl.pallas_call(
        functools.partial(resample_kernel, capacity),
        grid_spec=pltpu.PrefetchScalarGridSpec(
            num_scalar_prefetch=4,
            grid=(count // GROUP,),
            in_specs=[
                pl.BlockSpec((GROUP, 2, in_rows, width), lambda g, *_: (g, 0, 0, 0)),
                whole(*tables.shape),
                whole(*taps.shape),
            ],
            out_specs=[
                pl.BlockSpec((GROUP, 2, 8, width), lambda g, *_: (g, 0, 0, 0)),
                whole(tiles, rows, width),
                whole(tiles, 8, lanes),
            ],
            scratch_shapes=[
                pltpu.VMEM((GROUP * 16, 2 * width), jnp.bfloat16),
                pltpu.VMEM((GROUP * 64, GROUP * 16), jnp.bfloat16),
                pltpu.VMEM((GROUP * 64, 2 * width), jnp.float32),
                pltpu.SMEM((tiles,), jnp.int32),
            ],
        ),
        out_shape=[
            jax.ShapeDtypeStruct((count, 2, 8, width), jnp.bfloat16),
            jax.ShapeDtypeStruct((tiles, rows, width), jnp.bfloat16),
            jax.ShapeDtypeStruct((tiles, 8, lanes), jnp.int32),
        ],
        compiler_params=pltpu.CompilerParams(
            dimension_semantics=("arbitrary",), vmem_limit_bytes=40 * 1024 * 1024
        ),
        name="resample",
    )(target, block, row, col, pieces, tables, taps)


def exchange_kernel(
    n,
    length_ref,
    message_ref,
    lines_ref,
    tile_ref,
    out_ref,
    sum_ref,
    got,
    got_lines,
    total,
    tail,
    previous,
    own_sem,
    send_sem,
    recv_sem,
    lines_send_sem,
    lines_recv_sem,
    tail_sem,
):
    me = lax.axis_index("az")
    height = tile_ref.shape[1]
    rows = message_ref.shape[1]

    def own(part):
        if part:
            return pltpu.make_async_copy(lines_ref.at[me], got_lines.at[0], own_sem.at[1])
        return pltpu.make_async_copy(message_ref.at[me], got.at[0], own_sem.at[0])

    def data_copy(k):
        to = lax.rem(me + k, n)
        return pltpu.make_async_remote_copy(
            src_ref=message_ref.at[to],
            dst_ref=got.at[k],
            send_sem=send_sem.at[k],
            recv_sem=recv_sem.at[k],
            device_id={"az": to},
            device_id_type=MESH,
        )

    def lines_copy(k):
        to = lax.rem(me + k, n)
        return pltpu.make_async_remote_copy(
            src_ref=lines_ref.at[to],
            dst_ref=got_lines.at[k],
            send_sem=lines_send_sem.at[k],
            recv_sem=lines_recv_sem.at[k],
            device_id={"az": to},
            device_id_type=MESH,
        )

    own(0).start()
    own(1).start()
    barrier = pltpu.get_barrier_semaphore()

    @pl.loop(1, n)
    def _(k):
        pl.semaphore_signal(
            barrier, inc=1, device_id={"az": lax.rem(me + k, n)}, device_id_type=MESH
        )

    pl.semaphore_wait(barrier, n - 1)

    @pl.loop(1, n)
    def _(k):
        lines_copy(k).start()
        data_copy(k).start()

    wanted = lax.broadcasted_iota(jnp.int32, (2 * height, rows), 0)

    def placed(k):
        pick = (wanted == got_lines[k, 0:1, 0:rows]).astype(jnp.bfloat16)
        return jnp.dot(pick, got[k], preferred_element_type=jnp.float32)

    own(0).wait()
    own(1).wait()
    total[...] = placed(0)

    @pl.loop(1, n)
    def _(k):
        lines_copy(k).wait_recv()
        data_copy(k).wait_recv()
        total[...] += placed(k)

    ref_real, ref_imag = tile_ref[0], tile_ref[1]
    got_real, got_imag = total[0:height, :], total[height : 2 * height, :]
    out_ref[0] = ref_real * got_real + ref_imag * got_imag
    out_ref[1] = ref_imag * got_real - ref_real * got_imag
    tail[...] = out_ref[:, height - INTERSECTION : height, :]
    tail_copy = pltpu.make_async_remote_copy(
        src_ref=tail,
        dst_ref=previous,
        send_sem=tail_sem.at[0],
        recv_sem=tail_sem.at[1],
        device_id={"az": lax.rem(me + 1, n)},
        device_id_type=MESH,
    )
    tail_copy.start()
    length = length_ref[0]
    apart = lax.broadcasted_iota(
        jnp.int32, (INTERSECTION, INTERSECTION), 1
    ) - lax.broadcasted_iota(jnp.int32, (INTERSECTION, INTERSECTION), 0)
    shifter = (apart == INTERSECTION - length).astype(jnp.float32)
    tail_copy.wait_recv()
    before = [
        jnp.dot(
            shifter,
            previous[z],
            precision=lax.Precision.HIGHEST,
            preferred_element_type=jnp.float32,
        )
        for z in range(2)
    ]
    head = [out_ref[z, 0:INTERSECTION, :] for z in range(2)]
    scale = jnp.where(me == 0, 0.0, 1.0) / length.astype(jnp.float32)
    sum_ref[0, 0:1, :] = scale * jnp.sum(
        head[0] * before[0] + head[1] * before[1], axis=0, keepdims=True
    )
    sum_ref[0, 1:2, :] = scale * jnp.sum(
        head[1] * before[0] - head[0] * before[1], axis=0, keepdims=True
    )

    @pl.loop(1, n)
    def _(k):
        lines_copy(k).wait_send()
        data_copy(k).wait_send()

    tail_copy.wait_send()


def exchange(message, lines, tile, length):
    n, rows, width = message.shape
    height = tile.shape[1]
    return pl.pallas_call(
        functools.partial(exchange_kernel, n),
        in_specs=[
            pl.BlockSpec(memory_space=pltpu.SMEM),
            pl.BlockSpec(memory_space=pl.ANY),
            pl.BlockSpec(memory_space=pl.ANY),
            pl.BlockSpec(memory_space=pltpu.VMEM),
        ],
        out_specs=[pl.BlockSpec(memory_space=pltpu.VMEM)] * 2,
        out_shape=[
            jax.ShapeDtypeStruct(tile.shape, jnp.float32),
            jax.ShapeDtypeStruct((1, 2, width), jnp.float32),
        ],
        scratch_shapes=[
            pltpu.VMEM((n, rows, width), jnp.bfloat16),
            pltpu.VMEM(lines.shape, jnp.int32),
            pltpu.VMEM((2 * height, width), jnp.float32),
            pltpu.VMEM((2, INTERSECTION, width), jnp.float32),
            pltpu.VMEM((2, INTERSECTION, width), jnp.float32),
            pltpu.SemaphoreType.DMA((2,)),
            pltpu.SemaphoreType.DMA((n,)),
            pltpu.SemaphoreType.DMA((n,)),
            pltpu.SemaphoreType.DMA((n,)),
            pltpu.SemaphoreType.DMA((n,)),
            pltpu.SemaphoreType.DMA((2,)),
        ],
        compiler_params=pltpu.CompilerParams(
            collective_id=0, has_side_effects=True, vmem_limit_bytes=40 * 1024 * 1024
        ),
        name="exchange",
    )(length, message, lines, tile)


def tap_table(sinc_blocks):
    blocks = sinc_blocks.shape[0]
    a = jnp.arange(8)[:, None, None]
    r = jnp.arange(8)[None, :, None]
    q = jnp.arange(GROUP * 16)[None, None, :] % 16
    place = (q == r + a).astype(jnp.bfloat16)
    taps = jnp.einsum(
        "nab,arq->nbrq",
        sinc_blocks.astype(jnp.bfloat16),
        place,
        preferred_element_type=jnp.float32,
    ).astype(jnp.bfloat16)
    return taps.reshape(blocks, 64, GROUP * 16)


def on_device(
    secondary_pieces,
    piece_target,
    piece_block,
    piece_row,
    piece_column,
    ramp_rate,
    centroid,
    sinc_blocks,
    reference_tile,
    intersection_rows,
):
    tile_count = lax.axis_size("az")
    capacity = max(2, 2 * secondary_pieces.shape[0] // tile_count)
    tables = lax.all_gather(jnp.stack([ramp_rate, centroid], axis=1), "az", tiled=True)
    coregistered, message, lines = resample(
        secondary_pieces,
        piece_target[:, 0],
        piece_block,
        piece_row,
        piece_column,
        tables,
        tap_table(sinc_blocks),
        capacity,
    )
    interferogram, diversity = exchange(message, lines, reference_tile, intersection_rows)
    return coregistered, interferogram, diversity


def solution(mesh):
    split = ("dates", "az")
    return jax.shard_map(
        on_device,
        mesh=mesh,
        in_specs=(
            P(split, None, None, None),
            P(split, None),
            P(split),
            P(split),
            P(split),
            P(split, None),
            P(split, None),
            P(),
            P(None, split, None),
            P(split),
        ),
        out_specs=(
            P(split, None, None, None),
            P(None, split, None),
            P(split, None, None),
        ),
        check_vma=False,
    )
```

time: 474 us -> 105 us (0.22)
  the two profiles are of different devices: /device:TPU:12 before, /device:TPU:0 now
where the time goes in v1:
time: 105 us
  Pallas kernels  76.3 us (73%)
  blocking collectives  23.1 us (22%)
  local copies, waits for them, and re-layouts  2.61 us (2%)
  between operations  1.41 us (1%)
    pallas_call x1, Pallas kernels, exchange(): pl.pallas_call(functools.partial(exchange_kernel, n), in_specs=[pl.BlockS...  58.6 us
    all_gather x1, blocking collectives, on_device(): lax.all_gather(jnp.stack([ramp_rate, centroid], axis=1), 'az', tiled=True)  23.1 us
    pallas_call x1, Pallas kernels, resample(): pl.pallas_call(functools.partial(resample_kernel, capacity), grid_spec=pl...  17.8 us

profile of v1, /device:TPU:0, one launch (start us, length us, event | category | flops | bytes accessed | tf_op | source)
XLA Modules:
  0.0 105.0 jit_solution(3641251512843302602)
XLA Ops:
  0.6 0.8 convert_element_type.10
  1.4 0.8 convert_bitcast_fusion
  2.2 0.0 copy-start.6
  2.2 0.0 copy-start.7
  2.2 0.0 copy-start
  2.2 0.0 copy-start.2
  2.2 0.0 copy-start.3
  2.2 0.0 copy-start.4
  2.3 0.0 copy-start.5
  2.3 1.2 %copy.23 = bf16[64,8,8,256]{3,2,1,0:T(8,128)(2,1)S(1)} copy(bf16[64,8,8,256]{3,0,1,2:T(8,128)(2,1)S(1)} %convert_bitcast_fusion) | data formatting | bytes 4194304 | tf_op jit(solution)/shard_map/convert_element_type | solution.py:354
  3.5 0.0 copy-done.6
  3.5 0.0 copy-done.7
  3.5 23.1 %all_gather.3.table_ref = f32[16,2,256]{2,1,0:T(2,128)S(1)} all-gather(f32[1,2,256]{2,1,0:T(2,128)S(1)} %pad_maximum_fusion), channel_id=1, replica_groups=mesh['dates'=2,'az'=16] {'az'}, dimensions={0}, use_global_device_ids=true | all-gather | bytes 34816 | tf_op jit(solution)/shard_map/all_gather | solution.py:372
  26.6 0.0 copy-done
  26.6 0.0 copy-done.2
  26.6 0.0 copy-done.3
  26.6 0.0 copy-done.4
  26.6 0.0 copy-done.5
  26.7 0.0 copy-start.1
  26.7 17.8 %resample.1 = (bf16[128,2,8,256]{3,2,1,0:T(8,128)(2,1)}, bf16[16,256,256]{2,1,0:T(8,128)(2,1)S(1)}, s32[16,8,256]{2,1,0:T(8,128)S(1)}) custom-call(s32[128]{0:T(128)S(1)} %bitcast.17, s32[128]{0:T(128)S(1)} %copy-done.3, s32[128]{0:T(128)S(1)} %copy-done.4, s32[128]{0:T(128)S(1)} %copy-done.5, bf16[128,2,16,256]{3,2,1,0:T(8,128)(2,1)S(1)} %copy-done, ...), custom_call_target="tpu_custom_call" | custom-call | tf_op jit(solution)/shard_map/resample/pallas_call | solution.py:143
  45.1 0.0 copy-done.1
  45.1 58.6 %exchange.1 = (f32[2,256,256]{2,1,0:T(8,128)S(1)}, f32[1,2,256]{2,1,0:T(2,128)S(1)}) custom-call(s32[1]{0:T(128)S(6)} %copy.26.length_ref, bf16[16,256,256]{2,1,0:T(8,128)(2,1)S(1)} %get-tuple-element.9.message_ref, s32[16,8,256]{2,1,0:T(8,128)S(1)} %get-tuple-element.10.lines_ref, f32[2,256,256]{2,1,0:T(8,128)S(1)} %copy-done.1), custom_call_target="tpu_custom_call" | custom-call | tf_op jit(solution)/shard_map/exchange/pallas_call | solution.py:310
  103.7 0.8 copy.27
  104.5 0.6 copy.28
  (3 shorter events, 0.0 us)
Async XLA Ops:
  2.2 1.3 %copy-start.6 = (f32[1,256]{1,0:T(1,128)S(1)}, f32[1,256]{1,0:T(1,128)}, u32[]{:S(2)}) copy-start(f32[1,256]{1,0:T(1,128)} %param.16) | copy-start | bytes 3076
  2.2 1.3 %copy-start.7 = (f32[1,256]{1,0:T(1,128)S(1)}, f32[1,256]{1,0:T(1,128)}, u32[]{:S(2)}) copy-start(f32[1,256]{1,0:T(1,128)} %param.15) | copy-start | bytes 3076
  2.2 24.4 %copy-start = (bf16[128,2,16,256]{3,2,1,0:T(8,128)(2,1)S(1)}, bf16[128,2,16,256]{3,2,1,0:T(8,128)(2,1)}, u32[]{:S(2)}) copy-start(bf16[128,2,16,256]{3,2,1,0:T(8,128)(2,1)} %x_ref.1) | copy-start | bytes 6291460
  2.2 24.4 %copy-start.2 = (s32[128,1]{0,1:T(1,128)S(1)}, s32[128,1]{0,1:T(1,128)}, u32[]{:S(2)}) copy-start(s32[128,1]{0,1:T(1,128)} %param.11) | copy-start | bytes 1540
  2.2 24.4 %copy-start.3 = (s32[128]{0:T(128)S(1)}, s32[128]{0:T(128)}, u32[]{:S(2)}) copy-start(s32[128]{0:T(128)} %block.1) | copy-start | bytes 1540
  2.2 24.4 %copy-start.4 = (s32[128]{0:T(128)S(1)}, s32[128]{0:T(128)}, u32[]{:S(2)}) copy-start(s32[128]{0:T(128)} %row.1) | copy-start | bytes 1540
  2.3 24.4 %copy-start.5 = (s32[128]{0:T(128)S(1)}, s32[128]{0:T(128)}, u32[]{:S(2)}) copy-start(s32[128]{0:T(128)} %col.1) | copy-start | bytes 1540
  26.7 18.4 %copy-start.1 = (f32[2,256,256]{2,1,0:T(8,128)S(1)}, f32[2,256,256]{2,1,0:T(8,128)}, u32[]{:S(2)}) copy-start(f32[2,256,256]{2,1,0:T(8,128)} %tile_ref.1) | copy-start | bytes 1572868

commit v2 on v1

--- a/solution.py
+++ b/solution.py
@@ -11,6 +11,7 @@
 INTERSECTION = 32
 WEIGHT_BLOCKS = 64
 GROUP = 16
+MATES = 4
 MESH = pl.DeviceIdType.MESH
 
 SIN_FIT = (6.2831807136535645, -41.33925247192383, 81.40833282470703, -71.61119079589844)
@@ -126,8 +127,9 @@
         message_ref[tile, pl.ds(pl.multiple_of(slot * 16, 16), 16), :] = jnp.concatenate(
             [out_real, out_imag], axis=0
         ).astype(jnp.bfloat16)
-        lines_ref[tile, 0:1, :] = jnp.where(
-            slot_lane // 16 == slot, slot_line + row[p], lines_ref[tile, 0:1, :]
+        mate, plane = lax.rem(tile, MATES), pl.ds(tile // MATES, 1)
+        lines_ref[mate, plane, :] = jnp.where(
+            slot_lane // 16 == slot, slot_line + row[p], lines_ref[mate, plane, :]
         )
         return 0
 
@@ -138,7 +140,7 @@
     count, _, in_rows, width = pieces.shape
     tiles = tables.shape[0]
     rows = capacity * 16
-    lanes = max(128, rows)
+    line_shape = (MATES, max(8, tiles // MATES), max(128, rows))
     whole = lambda *shape: pl.BlockSpec(shape, lambda g, *_: (0,) * len(shape))
     return pl.pallas_call(
         functools.partial(resample_kernel, capacity),
@@ -153,7 +155,7 @@
             out_specs=[
                 pl.BlockSpec((GROUP, 2, 8, width), lambda g, *_: (g, 0, 0, 0)),
                 whole(tiles, rows, width),
-                whole(tiles, 8, lanes),
+                whole(*line_shape),
             ],
             scratch_shapes=[
                 pltpu.VMEM((GROUP * 16, 2 * width), jnp.bfloat16),
@@ -165,13 +167,122 @@
         out_shape=[
             jax.ShapeDtypeStruct((count, 2, 8, width), jnp.bfloat16),
             jax.ShapeDtypeStruct((tiles, rows, width), jnp.bfloat16),
-            jax.ShapeDtypeStruct((tiles, 8, lanes), jnp.int32),
+            jax.ShapeDtypeStruct(line_shape, jnp.int32),
         ],
         compiler_params=pltpu.CompilerParams(
             dimension_semantics=("arbitrary",), vmem_limit_bytes=40 * 1024 * 1024
         ),
         name="resample",
     )(target, block, row, col, pieces, tables, taps)
+
+
+def gather_kernel(n, rate_ref, centre_ref, sinc_ref, out_ref, taps_ref, own, got, wide, send_sem, recv_sem):
+    me = lax.axis_index("az")
+    barrier = pltpu.get_barrier_semaphore()
+
+    def to_all(k):
+        to = lax.rem(me + k, n)
+        return pltpu.make_async_remote_copy(
+            src_ref=own,
+            dst_ref=got.at[me],
+            send_sem=send_sem.at[k],
+            recv_sem=recv_sem.at[k],
+            device_id={"az": to},
+            device_id_type=MESH,
+        )
+
+    def from_all(k):
+        return pltpu.make_async_remote_copy(
+            src_ref=own,
+            dst_ref=got.at[lax.rem(me - k + n, n)],
+            send_sem=send_sem.at[k],
+            recv_sem=recv_sem.at[k],
+            device_id={"az": lax.rem(me + k, n)},
+            device_id_type=MESH,
+        )
+
+    @pl.loop(1, n)
+    def _(k):
+        pl.semaphore_signal(
+            barrier, inc=1, device_id={"az": lax.rem(me + k, n)}, device_id_type=MESH
+        )
+
+    own[0:1, :] = rate_ref[...]
+    own[1:2, :] = centre_ref[...]
+    got[me] = own[...]
+    pl.semaphore_wait(barrier, n - 1)
+
+    @pl.loop(1, n)
+    def _(k):
+        to_all(k).start()
+
+    blocks = sinc_ref.shape[2]
+    place = (
+        lax.broadcasted_iota(jnp.int32, (8, 128), 1) % 16
+        == lax.broadcasted_iota(jnp.int32, (8, 128), 0)
+    ).astype(jnp.float32)
+    for b in range(8):
+        wide[b] = lax.dot_general(
+            sinc_ref[b],
+            place,
+            (((0,), (0,)), ((), ())),
+            preferred_element_type=jnp.float32,
+        )
+
+    @pl.loop(0, blocks)
+    def _(block):
+        for b in range(0, 8, 2):
+            pair = jnp.concatenate(
+                [
+                    pltpu.roll(
+                        jnp.broadcast_to(wide[b + e, pl.ds(block, 1), :], (8, 128)),
+                        0,
+                        1,
+                        stride=1,
+                        stride_axis=0,
+                    )
+                    for e in range(2)
+                ],
+                axis=0,
+            ).astype(jnp.bfloat16)
+            for half in range(0, GROUP * 16, 128):
+                taps_ref[block, b * 8 : b * 8 + 16, half : half + 128] = pair
+
+    @pl.loop(1, n)
+    def _(k):
+        from_all(k).wait_recv()
+
+    out_ref[...] = got[...]
+
+    @pl.loop(1, n)
+    def _(k):
+        to_all(k).wait_send()
+
+
+def gather_tables(rate, centre, sinc_blocks):
+    n = lax.axis_size("az")
+    width = rate.shape[1]
+    blocks = sinc_blocks.shape[0]
+    return pl.pallas_call(
+        functools.partial(gather_kernel, n),
+        in_specs=[pl.BlockSpec(memory_space=pltpu.VMEM)] * 3,
+        out_specs=[pl.BlockSpec(memory_space=pltpu.VMEM)] * 2,
+        out_shape=[
+            jax.ShapeDtypeStruct((n, 2, width), jnp.float32),
+            jax.ShapeDtypeStruct((blocks, 64, GROUP * 16), jnp.bfloat16),
+        ],
+        scratch_shapes=[
+            pltpu.VMEM((2, width), jnp.float32),
+            pltpu.VMEM((n, 2, width), jnp.float32),
+            pltpu.VMEM((8, blocks, 128), jnp.float32),
+            pltpu.SemaphoreType.DMA((n,)),
+            pltpu.SemaphoreType.DMA((n,)),
+        ],
+        compiler_params=pltpu.CompilerParams(
+            collective_id=1, has_side_effects=True, vmem_limit_bytes=32 * 1024 * 1024
+        ),
+        name="gather_tables",
+    )(rate, centre, jnp.transpose(sinc_blocks, (2, 1, 0)))
 
 
 def exchange_kernel(
@@ -184,85 +295,62 @@
     sum_ref,
     got,
     got_lines,
+    part,
+    got_part,
     total,
     tail,
     previous,
-    own_sem,
     send_sem,
     recv_sem,
     lines_send_sem,
     lines_recv_sem,
+    part_send_sem,
+    part_recv_sem,
     tail_sem,
 ):
     me = lax.axis_index("az")
     height = tile_ref.shape[1]
     rows = message_ref.shape[1]
-
-    def own(part):
-        if part:
-            return pltpu.make_async_copy(lines_ref.at[me], got_lines.at[0], own_sem.at[1])
-        return pltpu.make_async_copy(message_ref.at[me], got.at[0], own_sem.at[0])
-
-    def data_copy(k):
-        to = lax.rem(me + k, n)
+    m = n // MATES
+    high, low = me // MATES, lax.rem(me, MATES)
+
+    def mate(e):
+        return high * MATES + lax.rem(low + e, MATES)
+
+    def peer(k):
+        return lax.rem(high + k, m) * MATES + low
+
+    def lines_copy(e):
         return pltpu.make_async_remote_copy(
-            src_ref=message_ref.at[to],
-            dst_ref=got.at[k],
-            send_sem=send_sem.at[k],
-            recv_sem=recv_sem.at[k],
-            device_id={"az": to},
+            src_ref=lines_ref.at[lax.rem(low + e, MATES)],
+            dst_ref=got_lines.at[e],
+            send_sem=lines_send_sem.at[e],
+            recv_sem=lines_recv_sem.at[e],
+            device_id={"az": mate(e)},
             device_id_type=MESH,
         )
 
-    def lines_copy(k):
-        to = lax.rem(me + k, n)
+    def data_copy(k, e):
+        tile = lax.rem(high + k, m) * MATES + lax.rem(low + e, MATES)
         return pltpu.make_async_remote_copy(
-            src_ref=lines_ref.at[to],
-            dst_ref=got_lines.at[k],
-            send_sem=lines_send_sem.at[k],
-            recv_sem=lines_recv_sem.at[k],
-            device_id={"az": to},
+            src_ref=message_ref.at[tile],
+            dst_ref=got.at[k, e],
+            send_sem=send_sem.at[k, e],
+            recv_sem=recv_sem.at[k, e],
+            device_id={"az": mate(e)},
             device_id_type=MESH,
         )
 
-    own(0).start()
-    own(1).start()
-    barrier = pltpu.get_barrier_semaphore()
-
-    @pl.loop(1, n)
-    def _(k):
-        pl.semaphore_signal(
-            barrier, inc=1, device_id={"az": lax.rem(me + k, n)}, device_id_type=MESH
-        )
-
-    pl.semaphore_wait(barrier, n - 1)
-
-    @pl.loop(1, n)
-    def _(k):
-        lines_copy(k).start()
-        data_copy(k).start()
-
-    wanted = lax.broadcasted_iota(jnp.int32, (2 * height, rows), 0)
-
-    def placed(k):
-        pick = (wanted == got_lines[k, 0:1, 0:rows]).astype(jnp.bfloat16)
-        return jnp.dot(pick, got[k], preferred_element_type=jnp.float32)
-
-    own(0).wait()
-    own(1).wait()
-    total[...] = placed(0)
-
-    @pl.loop(1, n)
-    def _(k):
-        lines_copy(k).wait_recv()
-        data_copy(k).wait_recv()
-        total[...] += placed(k)
-
-    ref_real, ref_imag = tile_ref[0], tile_ref[1]
-    got_real, got_imag = total[0:height, :], total[height : 2 * height, :]
-    out_ref[0] = ref_real * got_real + ref_imag * got_imag
-    out_ref[1] = ref_imag * got_real - ref_real * got_imag
-    tail[...] = out_ref[:, height - INTERSECTION : height, :]
+    def part_copy(k):
+        return pltpu.make_async_remote_copy(
+            src_ref=part.at[k],
+            dst_ref=got_part.at[k],
+            send_sem=part_send_sem.at[k],
+            recv_sem=part_recv_sem.at[k],
+            device_id={"az": peer(k)},
+            device_id_type=MESH,
+        )
+
     tail_copy = pltpu.make_async_remote_copy(
         src_ref=tail,
         dst_ref=previous,
@@ -271,13 +359,92 @@
         device_id={"az": lax.rem(me + 1, n)},
         device_id_type=MESH,
     )
-    tail_copy.start()
+
+    barrier = pltpu.get_barrier_semaphore()
+    for e in range(1, MATES):
+        pl.semaphore_signal(barrier, inc=1, device_id={"az": mate(e)}, device_id_type=MESH)
+
+    @pl.loop(1, m)
+    def _(k):
+        pl.semaphore_signal(barrier, inc=1, device_id={"az": peer(k)}, device_id_type=MESH)
+
+    @pl.when(low == 0)
+    def _():
+        pl.semaphore_signal(
+            barrier, inc=1, device_id={"az": lax.rem(me + n - 1, n)}, device_id_type=MESH
+        )
+
+    @pl.when(me == 0)
+    def _():
+        previous[...] = jnp.zeros_like(previous)
+
+    pl.semaphore_wait(barrier, MATES - 1 + m - 1 + low // (MATES - 1))
+
+    for e in range(1, MATES):
+        lines_copy(e).start()
+
+    def order(j):
+        return 1 + lax.rem(j + m // 2 - 1, m - 1) if m > 1 else 0
+
+    @pl.loop(0, m - 1)
+    def _(j):
+        for e in range(1, MATES):
+            data_copy(order(j), e).start()
+
+    for e in range(1, MATES):
+        data_copy(0, e).start()
+
+    wanted = lax.broadcasted_iota(jnp.int32, (2 * height, rows), 0)
+
+    def placed(lines, data):
+        pick = (wanted == lines).astype(jnp.bfloat16)
+        return jnp.dot(pick, data, preferred_element_type=jnp.float32)
+
+    def summed(k):
+        plane = lax.rem(high + k, m)
+        result = placed(lines_ref[low, pl.ds(plane, 1), 0:rows], message_ref[peer(k)])
+        for e in range(1, MATES):
+            data_copy(k, e).wait_recv()
+            result = result + placed(got_lines[e, pl.ds(plane, 1), 0:rows], got[k, e])
+        return result
+
+    for e in range(1, MATES):
+        lines_copy(e).wait_recv()
+
+    @pl.loop(0, m - 1)
+    def _(j):
+        k = order(j)
+        part[k] = summed(k).astype(jnp.bfloat16)
+        part_copy(k).start()
+
+    total[...] = summed(0)
+
+    @pl.loop(0, m - 1)
+    def _(j):
+        k = order(j)
+        part_copy(k).wait_recv()
+        total[...] += got_part[k].astype(jnp.float32)
+
+    ref_real, ref_imag = tile_ref[0], tile_ref[1]
+    got_real, got_imag = total[0:height, :], total[height : 2 * height, :]
+    out_ref[0] = ref_real * got_real + ref_imag * got_imag
+    out_ref[1] = ref_imag * got_real - ref_real * got_imag
+    tail[...] = out_ref[:, height - INTERSECTION : height, :]
+
+    @pl.when(me < n - 1)
+    def _():
+        tail_copy.start()
+
     length = length_ref[0]
     apart = lax.broadcasted_iota(
         jnp.int32, (INTERSECTION, INTERSECTION), 1
     ) - lax.broadcasted_iota(jnp.int32, (INTERSECTION, INTERSECTION), 0)
     shifter = (apart == INTERSECTION - length).astype(jnp.float32)
-    tail_copy.wait_recv()
+
+    @pl.when(me > 0)
+    def _():
+        tail_copy.wait_recv()
+
     before = [
         jnp.dot(
             shifter,
@@ -288,7 +455,7 @@
         for z in range(2)
     ]
     head = [out_ref[z, 0:INTERSECTION, :] for z in range(2)]
-    scale = jnp.where(me == 0, 0.0, 1.0) / length.astype(jnp.float32)
+    scale = 1.0 / length.astype(jnp.float32)
     sum_ref[0, 0:1, :] = scale * jnp.sum(
         head[0] * before[0] + head[1] * before[1], axis=0, keepdims=True
     )
@@ -296,63 +463,58 @@
         head[1] * before[0] - head[0] * before[1], axis=0, keepdims=True
     )
 
-    @pl.loop(1, n)
-    def _(k):
-        lines_copy(k).wait_send()
-        data_copy(k).wait_send()
-
-    tail_copy.wait_send()
+    for e in range(1, MATES):
+        lines_copy(e).wait_send()
+
+    @pl.loop(0, m)
+    def _(k):
+        for e in range(1, MATES):
+            data_copy(k, e).wait_send()
+
+    @pl.loop(1, m)
+    def _(k):
+        part_copy(k).wait_send()
+
+    @pl.when(me < n - 1)
+    def _():
+        tail_copy.wait_send()
 
 
 def exchange(message, lines, tile, length):
     n, rows, width = message.shape
     height = tile.shape[1]
+    m = n // MATES
+    dma = pltpu.SemaphoreType.DMA
     return pl.pallas_call(
         functools.partial(exchange_kernel, n),
-        in_specs=[
-            pl.BlockSpec(memory_space=pltpu.SMEM),
-            pl.BlockSpec(memory_space=pl.ANY),
-            pl.BlockSpec(memory_space=pl.ANY),
-            pl.BlockSpec(memory_space=pltpu.VMEM),
-        ],
+        in_specs=[pl.BlockSpec(memory_space=pltpu.SMEM)]
+        + [pl.BlockSpec(memory_space=pltpu.VMEM)] * 3,
         out_specs=[pl.BlockSpec(memory_space=pltpu.VMEM)] * 2,
         out_shape=[
             jax.ShapeDtypeStruct(tile.shape, jnp.float32),
             jax.ShapeDtypeStruct((1, 2, width), jnp.float32),
         ],
         scratch_shapes=[
-            pltpu.VMEM((n, rows, width), jnp.bfloat16),
+            pltpu.VMEM((m, MATES, rows, width), jnp.bfloat16),
             pltpu.VMEM(lines.shape, jnp.int32),
+            pltpu.VMEM((m, 2 * height, width), jnp.bfloat16),
+            pltpu.VMEM((m, 2 * height, width), jnp.bfloat16),
             pltpu.VMEM((2 * height, width), jnp.float32),
             pltpu.VMEM((2, INTERSECTION, width), jnp.float32),
             pltpu.VMEM((2, INTERSECTION, width), jnp.float32),
-            pltpu.SemaphoreType.DMA((2,)),
-            pltpu.SemaphoreType.DMA((n,)),
-            pltpu.SemaphoreType.DMA((n,)),
-            pltpu.SemaphoreType.DMA((n,)),
-            pltpu.SemaphoreType.DMA((n,)),
-            pltpu.SemaphoreType.DMA((2,)),
+            dma((m, MATES)),
+            dma((m, MATES)),
+            dma((MATES,)),
+            dma((MATES,)),
+            dma((m,)),
+            dma((m,)),
+            dma((2,)),
         ],
         compiler_params=pltpu.CompilerParams(
-            collective_id=0, has_side_effects=True, vmem_limit_bytes=40 * 1024 * 1024
+            collective_id=0, has_side_effects=True, vmem_limit_bytes=48 * 1024 * 1024
         ),
         name="exchange",
     )(length, message, lines, tile)
-
-
-def tap_table(sinc_blocks):
-    blocks = sinc_blocks.shape[0]
-    a = jnp.arange(8)[:, None, None]
-    r = jnp.arange(8)[None, :, None]
-    q = jnp.arange(GROUP * 16)[None, None, :] % 16
-    place = (q == r + a).astype(jnp.bfloat16)
-    taps = jnp.einsum(
-        "nab,arq->nbrq",
-        sinc_blocks.astype(jnp.bfloat16),
-        place,
-        preferred_element_type=jnp.float32,
-    ).astype(jnp.bfloat16)
-    return taps.reshape(blocks, 64, GROUP * 16)
 
 
 def on_device(
@@ -369,7 +531,7 @@
 ):
     tile_count = lax.axis_size("az")
     capacity = max(2, 2 * secondary_pieces.shape[0] // tile_count)
-    tables = lax.all_gather(jnp.stack([ramp_rate, centroid], axis=1), "az", tiled=True)
+    tables, taps = gather_tables(ramp_rate, centroid, sinc_blocks)
     coregistered, message, lines = resample(
         secondary_pieces,
         piece_target[:, 0],
@@ -377,7 +539,7 @@
         piece_row,
         piece_column,
         tables,
-        tap_table(sinc_blocks),
+        taps,
         capacity,
     )
     interferogram, diversity = exchange(message, lines, reference_tile, intersection_rows)

time: 105 us -> 73.4 us (0.70)
  the two profiles are of different devices: /device:TPU:0 before, /device:TPU:12 now
where the time goes in v2:
time: 73.4 us; the launch traced here: 72.1 us
  Pallas kernels  63.1 us (86%)
  local copies, waits for them, and re-layouts  7.7 us (10%)
  between operations  1.32 us (2%)
    pallas_call x1, Pallas kernels, exchange(): pl.pallas_call(functools.partial(exchange_kernel, n), in_specs=[pl.BlockS...  35.5 us
    pallas_call x1, Pallas kernels, resample(): pl.pallas_call(functools.partial(resample_kernel, capacity), grid_spec=pl...  18.6 us
    pallas_call x1, Pallas kernels, gather_tables(): pl.pallas_call(functools.partial(gather_kernel, n), in_specs=[pl.BlockSpe...  9.06 us
    unnamed x19, local copies, waits for them, and re-layouts  7.7 us

profile of v2, /device:TPU:12, one launch (start us, length us, event | category | flops | bytes accessed | tf_op | source)
XLA Modules:
  0.0 72.1 jit_solution(15701637893962494402)
XLA Ops:
  0.6 0.8 %copy.15 = f32[64,8,8]{0,1,2:T(8,128)S(1)} copy(f32[64,8,8]{0,2,1:T(8,128)} %param.17) | data formatting | bytes 32768 | tf_op args[7]
  1.4 0.0 copy-start.2
  1.4 0.7 copy-done.2
  2.1 0.0 copy-start.3
  2.1 0.7 copy-done.3
  2.8 9.1 %gather_tables.1 = (f32[16,2,256]{2,1,0:T(2,128)S(1)}, bf16[64,64,256]{2,1,0:T(8,128)(2,1)S(1)}) custom-call(f32[1,256]{1,0:T(1,128)S(1)} %copy-done.2, f32[1,256]{1,0:T(1,128)S(1)} %copy-done.3, f32[8,8,64]{2,1,0:T(8,128)S(1)} %bitcast.4), custom_call_target="tpu_custom_call" | custom-call | tf_op jit(solution)/shard_map/gather_tables/pallas_call | solution.py:266
  11.8 0.0 copy-start
  11.8 1.6 %copy-done = bf16[128,2,16,256]{3,2,1,0:T(8,128)(2,1)S(1)} copy-done((bf16[128,2,16,256]{3,2,1,0:T(8,128)(2,1)S(1)}, bf16[128,2,16,256]{3,2,1,0:T(8,128)(2,1)}, u32[]{:S(2)}) %copy-start) | copy-done | bytes 2097176
  13.4 0.0 copy-start.4
  13.4 0.7 copy-done.4
  14.1 0.0 copy-start.5
  14.1 0.7 copy-done.5
  14.7 0.0 copy-start.6
  14.7 0.7 copy-done.6
  15.4 0.0 copy-start.7
  15.4 0.7 copy-done.7
  16.0 0.0 copy-start.1
  16.0 18.6 %resample.1 = (bf16[128,2,8,256]{3,2,1,0:T(8,128)(2,1)}, bf16[16,256,256]{2,1,0:T(8,128)(2,1)S(1)}, s32[4,8,256]{2,1,0:T(8,128)S(1)}) custom-call(s32[128]{0:T(128)S(1)} %bitcast.5, s32[128]{0:T(128)S(1)} %copy-done.5, s32[128]{0:T(128)S(1)} %copy-done.6, s32[128]{0:T(128)S(1)} %copy-done.7, bf16[128,2,16,256]{3,2,1,0:T(8,128)(2,1)S(1)} %copy-done, ...), custom_call_target="tpu_custom_call" | custom-call | tf_op jit(solution)/shard_map/resample/pallas_call | solution.py:145
  35.3 0.0 copy-done.1
  35.3 35.5 %exchange.1 = (f32[2,256,256]{2,1,0:T(8,128)S(1)}, f32[1,2,256]{2,1,0:T(2,128)S(1)}) custom-call(s32[1]{0:T(128)S(6)} %copy.18.length_ref, bf16[16,256,256]{2,1,0:T(8,128)(2,1)S(1)} %get-tuple-element.13.message_ref, s32[4,8,256]{2,1,0:T(8,128)S(1)} %get-tuple-element.14.lines_ref, f32[2,256,256]{2,1,0:T(8,128)S(1)} %copy-done.1), custom_call_target="tpu_custom_call" | custom-call | tf_op jit(solution)/shard_map/exchange/pallas_call | solution.py:488
  70.8 0.8 %copy.19 = f32[2,256,256]{2,1,0:T(8,128)} copy(f32[2,256,256]{2,1,0:T(8,128)S(1)} %get-tuple-element.21) | data formatting | bytes 1048576
  71.6 0.6 copy.20
Async XLA Ops:
  1.4 0.7 copy-start.2
  2.1 0.7 copy-start.3
  11.8 1.6 %copy-start = (bf16[128,2,16,256]{3,2,1,0:T(8,128)(2,1)S(1)}, bf16[128,2,16,256]{3,2,1,0:T(8,128)(2,1)}, u32[]{:S(2)}) copy-start(bf16[128,2,16,256]{3,2,1,0:T(8,128)(2,1)} %x_ref.1) | copy-start | bytes 6291460
  13.4 0.7 copy-start.4
  14.1 0.7 copy-start.5
  14.7 0.7 copy-start.6
  15.4 0.7 copy-start.7
  16.0 19.2 %copy-start.1 = (f32[2,256,256]{2,1,0:T(8,128)S(1)}, f32[2,256,256]{2,1,0:T(8,128)}, u32[]{:S(2)}) copy-start(f32[2,256,256]{2,1,0:T(8,128)} %tile_ref.1) | copy-start | bytes 1572868

commit v3 on v2

--- a/solution.py
+++ b/solution.py
@@ -11,7 +11,8 @@
 INTERSECTION = 32
 WEIGHT_BLOCKS = 64
 GROUP = 16
-MATES = 4
+MATES = 8
+VMEM_BYTES = 63 * 1024 * 1024
 MESH = pl.DeviceIdType.MESH
 
 SIN_FIT = (6.2831807136535645, -41.33925247192383, 81.40833282470703, -71.61119079589844)
@@ -32,14 +33,13 @@
 
 
 def resample_kernel(
-    capacity,
-    target,
-    block,
-    row,
-    col,
-    x_ref,
+    target_ref,
+    block_ref,
+    row_ref,
+    col_ref,
+    pieces_ref,
     table_ref,
-    taps_ref,
+    taps_hbm,
     out_ref,
     message_ref,
     lines_ref,
@@ -47,19 +47,57 @@
     band,
     mixed,
     used,
+    target,
+    block,
+    row,
+    col,
+    pieces,
+    taps_ref,
+    fetch_sem,
+    pieces_sem,
 ):
     step = pl.program_id(0)
-    width = x_ref.shape[3]
+    width = pieces_ref.shape[3]
     half = width // 2
+    fetches = [
+        pltpu.make_async_copy(source, scalars, fetch_sem.at[i])
+        for i, (source, scalars) in enumerate(
+            [
+                (target_ref, target),
+                (block_ref, block),
+                (row_ref, row),
+                (col_ref, col),
+                (taps_hbm, taps_ref),
+            ]
+        )
+    ]
+
+    def pieces_copy(group):
+        part = pl.ds(group * GROUP, GROUP)
+        return pltpu.make_async_copy(
+            pieces_ref.at[part], pieces.at[part], pieces_sem.at[group]
+        )
 
     @pl.when(step == 0)
     def _():
+        for fetch in fetches:
+            fetch.start()
+
+        @pl.loop(0, pieces_ref.shape[0] // GROUP)
+        def _(group):
+            pieces_copy(group).start()
+
         message_ref[...] = jnp.zeros_like(message_ref)
         lines_ref[...] = jnp.full_like(lines_ref, -1)
 
         @pl.loop(0, used.shape[0])
         def _(tile):
             used[tile] = 0
+
+        for fetch in fetches:
+            fetch.wait()
+
+    pieces_copy(step).wait()
 
     in_iota = lax.broadcasted_iota(jnp.int32, (16, width), 0).astype(jnp.float32)
     out_iota = lax.broadcasted_iota(jnp.int32, (8, width), 0).astype(jnp.float32)
@@ -69,15 +107,15 @@
     slot_line = (slot_lane % 16) // 8 * TILE_ROWS + slot_lane % 8
 
     def table_rows(tile):
-        return 0.5 * table_ref[tile, 0:1, :], table_ref[tile, 1:2, :]
+        return 0.5 * table_ref[tile, 0], table_ref[tile, 1]
 
     def before(i, _):
         p = step * GROUP + i
         rate, centre = table_rows(target[p])
         u = (in_iota + (row[p].astype(jnp.float32) - (3.0 + TILE_ROWS / 2))) * (1.0 / TILE_ROWS)
         cosine, sine = unit_phasor((rate * u + centre) * u)
-        real = x_ref[i, 0].astype(jnp.float32)
-        imag = x_ref[i, 1].astype(jnp.float32)
+        real = pieces[p, 0].astype(jnp.float32)
+        imag = pieces[p, 1].astype(jnp.float32)
         lines = pl.ds(pl.multiple_of(i * 16, 16), 16)
         deramped[lines, 0:width] = (real * cosine + imag * sine).astype(jnp.bfloat16)
         deramped[lines, width : 2 * width] = (imag * cosine - real * sine).astype(jnp.bfloat16)
@@ -137,23 +175,24 @@
 
 
 def resample(pieces, target, block, row, col, tables, taps, capacity):
-    count, _, in_rows, width = pieces.shape
+    count, _, _, width = pieces.shape
     tiles = tables.shape[0]
     rows = capacity * 16
     line_shape = (MATES, max(8, tiles // MATES), max(128, rows))
-    whole = lambda *shape: pl.BlockSpec(shape, lambda g, *_: (0,) * len(shape))
+    whole = lambda *shape: pl.BlockSpec(shape, lambda g: (0,) * len(shape))
+    remote = pl.BlockSpec(memory_space=pltpu.HBM)
     return pl.pallas_call(
-        functools.partial(resample_kernel, capacity),
+        resample_kernel,
         grid_spec=pltpu.PrefetchScalarGridSpec(
-            num_scalar_prefetch=4,
+            num_scalar_prefetch=0,
             grid=(count // GROUP,),
             in_specs=[
-                pl.BlockSpec((GROUP, 2, in_rows, width), lambda g, *_: (g, 0, 0, 0)),
+                *[remote] * 5,
                 whole(*tables.shape),
-                whole(*taps.shape),
+                remote,
             ],
             out_specs=[
-                pl.BlockSpec((GROUP, 2, 8, width), lambda g, *_: (g, 0, 0, 0)),
+                pl.BlockSpec((GROUP, 2, 8, width), lambda g: (g, 0, 0, 0)),
                 whole(tiles, rows, width),
                 whole(*line_shape),
             ],
@@ -162,6 +201,11 @@
                 pltpu.VMEM((GROUP * 64, GROUP * 16), jnp.bfloat16),
                 pltpu.VMEM((GROUP * 64, 2 * width), jnp.float32),
                 pltpu.SMEM((tiles,), jnp.int32),
+                *[pltpu.SMEM((count,), jnp.int32)] * 4,
+                pltpu.VMEM(pieces.shape, jnp.bfloat16),
+                pltpu.VMEM(taps.shape, jnp.bfloat16),
+                pltpu.SemaphoreType.DMA((5,)),
+                pltpu.SemaphoreType.DMA((count // GROUP,)),
             ],
         ),
         out_shape=[
@@ -170,14 +214,35 @@
             jax.ShapeDtypeStruct(line_shape, jnp.int32),
         ],
         compiler_params=pltpu.CompilerParams(
-            dimension_semantics=("arbitrary",), vmem_limit_bytes=40 * 1024 * 1024
+            dimension_semantics=("arbitrary",), vmem_limit_bytes=VMEM_BYTES
         ),
         name="resample",
     )(target, block, row, col, pieces, tables, taps)
 
 
-def gather_kernel(n, rate_ref, centre_ref, sinc_ref, out_ref, taps_ref, own, got, wide, send_sem, recv_sem):
+def gather_kernel(
+    n,
+    rate_ref,
+    centre_ref,
+    sinc_ref,
+    out_ref,
+    taps_ref,
+    own,
+    got,
+    sinc,
+    wide,
+    fetch_sem,
+    send_sem,
+    recv_sem,
+):
     me = lax.axis_index("az")
+    fetches = [
+        pltpu.make_async_copy(rate_ref, own.at[0], fetch_sem.at[0]),
+        pltpu.make_async_copy(centre_ref, own.at[1], fetch_sem.at[1]),
+        pltpu.make_async_copy(sinc_ref, sinc, fetch_sem.at[2]),
+    ]
+    for fetch in fetches:
+        fetch.start()
     barrier = pltpu.get_barrier_semaphore()
 
     def to_all(k):
@@ -207,8 +272,8 @@
             barrier, inc=1, device_id={"az": lax.rem(me + k, n)}, device_id_type=MESH
         )
 
-    own[0:1, :] = rate_ref[...]
-    own[1:2, :] = centre_ref[...]
+    fetches[0].wait()
+    fetches[1].wait()
     got[me] = own[...]
     pl.semaphore_wait(barrier, n - 1)
 
@@ -216,6 +281,7 @@
     def _(k):
         to_all(k).start()
 
+    fetches[2].wait()
     blocks = sinc_ref.shape[2]
     place = (
         lax.broadcasted_iota(jnp.int32, (8, 128), 1) % 16
@@ -223,7 +289,7 @@
     ).astype(jnp.float32)
     for b in range(8):
         wide[b] = lax.dot_general(
-            sinc_ref[b],
+            sinc[:, b, :],
             place,
             (((0,), (0,)), ((), ())),
             preferred_element_type=jnp.float32,
@@ -265,34 +331,39 @@
     blocks = sinc_blocks.shape[0]
     return pl.pallas_call(
         functools.partial(gather_kernel, n),
-        in_specs=[pl.BlockSpec(memory_space=pltpu.VMEM)] * 3,
+        in_specs=[pl.BlockSpec(memory_space=pltpu.HBM)] * 3,
         out_specs=[pl.BlockSpec(memory_space=pltpu.VMEM)] * 2,
         out_shape=[
-            jax.ShapeDtypeStruct((n, 2, width), jnp.float32),
+            jax.ShapeDtypeStruct((n, 2, 1, width), jnp.float32),
             jax.ShapeDtypeStruct((blocks, 64, GROUP * 16), jnp.bfloat16),
         ],
         scratch_shapes=[
-            pltpu.VMEM((2, width), jnp.float32),
-            pltpu.VMEM((n, 2, width), jnp.float32),
+            pltpu.VMEM((2, 1, width), jnp.float32),
+            pltpu.VMEM((n, 2, 1, width), jnp.float32),
+            pltpu.VMEM((8, 8, blocks), jnp.float32),
             pltpu.VMEM((8, blocks, 128), jnp.float32),
+            pltpu.SemaphoreType.DMA((3,)),
             pltpu.SemaphoreType.DMA((n,)),
             pltpu.SemaphoreType.DMA((n,)),
         ],
         compiler_params=pltpu.CompilerParams(
-            collective_id=1, has_side_effects=True, vmem_limit_bytes=32 * 1024 * 1024
+            collective_id=1, has_side_effects=True, vmem_limit_bytes=VMEM_BYTES
         ),
         name="gather_tables",
-    )(rate, centre, jnp.transpose(sinc_blocks, (2, 1, 0)))
+    )(rate, centre, jnp.transpose(sinc_blocks, (1, 2, 0)))
 
 
 def exchange_kernel(
     n,
     length_ref,
     message_ref,
+    lines_hbm,
+    tile_hbm,
+    out_ref,
+    sum_ref,
     lines_ref,
     tile_ref,
-    out_ref,
-    sum_ref,
+    own_sem,
     got,
     got_lines,
     part,
@@ -309,9 +380,13 @@
     tail_sem,
 ):
     me = lax.axis_index("az")
-    height = tile_ref.shape[1]
+    height = tile_hbm.shape[1]
     rows = message_ref.shape[1]
     m = n // MATES
+    lines_fetch = pltpu.make_async_copy(lines_hbm, lines_ref, own_sem.at[0])
+    tile_fetch = pltpu.make_async_copy(tile_hbm, tile_ref, own_sem.at[1])
+    lines_fetch.start()
+    tile_fetch.start()
     high, low = me // MATES, lax.rem(me, MATES)
 
     def mate(e):
@@ -341,6 +416,9 @@
             device_id_type=MESH,
         )
 
+    def own_copy(k):
+        return pltpu.make_async_copy(message_ref.at[peer(k)], got.at[k, 0], own_sem.at[2 + k])
+
     def part_copy(k):
         return pltpu.make_async_remote_copy(
             src_ref=part.at[k],
@@ -360,6 +438,10 @@
         device_id_type=MESH,
     )
 
+    @pl.loop(0, m)
+    def _(k):
+        own_copy(k).start()
+
     barrier = pltpu.get_barrier_semaphore()
     for e in range(1, MATES):
         pl.semaphore_signal(barrier, inc=1, device_id={"az": mate(e)}, device_id_type=MESH)
@@ -380,6 +462,7 @@
 
     pl.semaphore_wait(barrier, MATES - 1 + m - 1 + low // (MATES - 1))
 
+    lines_fetch.wait()
     for e in range(1, MATES):
         lines_copy(e).start()
 
@@ -402,7 +485,8 @@
 
     def summed(k):
         plane = lax.rem(high + k, m)
-        result = placed(lines_ref[low, pl.ds(plane, 1), 0:rows], message_ref[peer(k)])
+        own_copy(k).wait()
+        result = placed(lines_ref[low, pl.ds(plane, 1), 0:rows], got[k, 0])
         for e in range(1, MATES):
             data_copy(k, e).wait_recv()
             result = result + placed(got_lines[e, pl.ds(plane, 1), 0:rows], got[k, e])
@@ -425,6 +509,7 @@
         part_copy(k).wait_recv()
         total[...] += got_part[k].astype(jnp.float32)
 
+    tile_fetch.wait()
     ref_real, ref_imag = tile_ref[0], tile_ref[1]
     got_real, got_imag = total[0:height, :], total[height : 2 * height, :]
     out_ref[0] = ref_real * got_real + ref_imag * got_imag
@@ -488,13 +573,16 @@
     return pl.pallas_call(
         functools.partial(exchange_kernel, n),
         in_specs=[pl.BlockSpec(memory_space=pltpu.SMEM)]
-        + [pl.BlockSpec(memory_space=pltpu.VMEM)] * 3,
+        + [pl.BlockSpec(memory_space=pltpu.HBM)] * 3,
         out_specs=[pl.BlockSpec(memory_space=pltpu.VMEM)] * 2,
         out_shape=[
             jax.ShapeDtypeStruct(tile.shape, jnp.float32),
             jax.ShapeDtypeStruct((1, 2, width), jnp.float32),
         ],
         scratch_shapes=[
+            pltpu.VMEM(lines.shape, jnp.int32),
+            pltpu.VMEM(tile.shape, jnp.float32),
+            dma((2 + m,)),
             pltpu.VMEM((m, MATES, rows, width), jnp.bfloat16),
             pltpu.VMEM(lines.shape, jnp.int32),
             pltpu.VMEM((m, 2 * height, width), jnp.bfloat16),
@@ -511,7 +599,7 @@
             dma((2,)),
         ],
         compiler_params=pltpu.CompilerParams(
-            collective_id=0, has_side_effects=True, vmem_limit_bytes=48 * 1024 * 1024
+            collective_id=0, has_side_effects=True, vmem_limit_bytes=VMEM_BYTES
         ),
         name="exchange",
     )(length, message, lines, tile)

time: 73.4 us -> 74.5 us (1.015); the launches traced: 72.1 us -> 74.2 us
  Pallas kernels: 63.1 us -> 69.8 us
  local copies, waits for them, and re-layouts: 7.7 us -> 3.11 us
    unnamed x19 -> x2, local copies, waits for them, and re-layouts: 7.7 us -> 3.11 us
    pallas_call x1, Pallas kernels: 35.5 us -> 38.3 us  [exchange(): pl.pallas_call(functools.partial(exchange_kernel, n), in_specs=[pl.BlockS...]
    pallas_call x1, Pallas kernels: 18.6 us -> 21 us  [resample(): pl.pallas_call(resample_kernel, grid_spec=pltpu.PrefetchScalarGridSpec(nu...]
    pallas_call x1, Pallas kernels: 9.06 us -> 10.5 us  [gather_tables(): pl.pallas_call(functools.partial(gather_kernel, n), in_specs=[pl.BlockSpe...]
where the time goes in v3:
time: 74.5 us; the launch traced here: 74.2 us
  Pallas kernels  69.8 us (94%)
  local copies, waits for them, and re-layouts  3.11 us (4%)
  between operations  1.3 us (2%)
    pallas_call x1, Pallas kernels, exchange(): pl.pallas_call(functools.partial(exchange_kernel, n), in_specs=[pl.BlockS...  38.3 us
    pallas_call x1, Pallas kernels, resample(): pl.pallas_call(resample_kernel, grid_spec=pltpu.PrefetchScalarGridSpec(nu...  21 us
    pallas_call x1, Pallas kernels, gather_tables(): pl.pallas_call(functools.partial(gather_kernel, n), in_specs=[pl.BlockSpe...  10.5 us
    unnamed x2, local copies, waits for them, and re-layouts  3.11 us

profile of v3, /device:TPU:12, one launch (start us, length us, event | category | flops | bytes accessed | tf_op | source)
XLA Modules:
  0.0 74.2 jit_solution(15842754999436521393)
XLA Ops:
  0.6 10.5 %gather_tables.1 = (f32[16,2,1,256]{3,2,1,0:T(1,128)}, bf16[64,64,256]{2,1,0:T(8,128)(2,1)}) custom-call(f32[1,256]{1,0:T(1,128)} %rate_ref.1, f32[1,256]{1,0:T(1,128)} %centre_ref.1, f32[8,8,64]{2,1,0:T(8,128)} %bitcast.2), custom_call_target="tpu_custom_call" | custom-call | tf_op jit(solution)/shard_map/gather_tables/pallas_call | solution.py:332
  11.2 21.0 %resample.1 = (bf16[128,2,8,256]{3,2,1,0:T(8,128)(2,1)}, bf16[16,256,256]{2,1,0:T(8,128)(2,1)}, s32[8,8,256]{2,1,0:T(8,128)}) custom-call(s32[128]{0:T(128)} %bitcast.3, s32[128]{0:T(128)} %block_ref.1, s32[128]{0:T(128)} %row_ref.1, s32[128]{0:T(128)} %col_ref.1, bf16[128,2,16,256]{3,2,1,0:T(8,128)(2,1)} %pieces_ref.1, ...), custom_call_target="tpu_custom_call" | custom-call | tf_op jit(solution)/shard_map/resample/pallas_call | solution.py:184
  32.8 38.3 %exchange.1 = (f32[2,256,256]{2,1,0:T(8,128)}, f32[1,2,256]{2,1,0:T(2,128)}) custom-call(s32[1]{0:T(128)S(6)} %copy.15.length_ref, bf16[16,256,256]{2,1,0:T(8,128)(2,1)} %get-tuple-element.13.message_ref, s32[8,8,256]{2,1,0:T(8,128)} %get-tuple-element.14.lines_hbm, f32[2,256,256]{2,1,0:T(8,128)} %tile_hbm.1), custom_call_target="tpu_custom_call" | custom-call | tf_op jit(solution)/shard_map/exchange/pallas_call | solution.py:573
  71.1 1.9 %copy.16 = f32[2,256,256]{2,1,0:T(8,128)} copy(f32[2,256,256]{2,1,0:T(8,128)} %get-tuple-element.21) | data formatting | bytes 1048576
  73.0 1.2 %copy.17 = f32[1,2,256]{2,1,0:T(2,128)} copy(f32[1,2,256]{2,1,0:T(2,128)} %get-tuple-element.22) | data formatting | bytes 4096

commit v4 on v3

--- a/solution.py
+++ b/solution.py
@@ -88,6 +88,7 @@
             pieces_copy(group).start()
 
         message_ref[...] = jnp.zeros_like(message_ref)
+        band[...] = jnp.zeros_like(band)
         lines_ref[...] = jnp.full_like(lines_ref, -1)
 
         @pl.loop(0, used.shape[0])
@@ -101,34 +102,36 @@
 
     in_iota = lax.broadcasted_iota(jnp.int32, (16, width), 0).astype(jnp.float32)
     out_iota = lax.broadcasted_iota(jnp.int32, (8, width), 0).astype(jnp.float32)
-    band_lane = lax.broadcasted_iota(jnp.int32, (64, GROUP * 16), 1) // 16
+    band_lane = lax.broadcasted_iota(jnp.int32, (64, 128), 1) // 16
     lane = lax.broadcasted_iota(jnp.int32, (8, half), 1)
     slot_lane = lax.broadcasted_iota(jnp.int32, (1, lines_ref.shape[2]), 1)
-    slot_line = (slot_lane % 16) // 8 * TILE_ROWS + slot_lane % 8
+    slot_line = slot_lane % 8
 
     def table_rows(tile):
         return 0.5 * table_ref[tile, 0], table_ref[tile, 1]
 
-    def before(i, _):
+    def before(i):
         p = step * GROUP + i
         rate, centre = table_rows(target[p])
         u = (in_iota + (row[p].astype(jnp.float32) - (3.0 + TILE_ROWS / 2))) * (1.0 / TILE_ROWS)
         cosine, sine = unit_phasor((rate * u + centre) * u)
         real = pieces[p, 0].astype(jnp.float32)
         imag = pieces[p, 1].astype(jnp.float32)
-        lines = pl.ds(pl.multiple_of(i * 16, 16), 16)
+        lines = slice(i * 16, i * 16 + 16)
         deramped[lines, 0:width] = (real * cosine + imag * sine).astype(jnp.bfloat16)
         deramped[lines, width : 2 * width] = (imag * cosine - real * sine).astype(jnp.bfloat16)
         taps = taps_ref[block[p]]
-        band[pl.ds(pl.multiple_of(i * 64, 64), 64), :] = jnp.where(
-            band_lane == i, taps, jnp.zeros_like(taps)
-        )
-        return 0
-
-    lax.fori_loop(0, GROUP, before, 0, unroll=4)
+        first = i // 8 * 128
+        band[i * 64 : i * 64 + 64, first : first + 128] = jnp.where(
+            band_lane == i % 8, taps, jnp.zeros_like(taps)
+        )
+
+    for i in range(GROUP):
+        before(i)
+
     mixed[...] = jnp.dot(band[...], deramped[...], preferred_element_type=jnp.float32)
 
-    def after(i, _):
+    def after(i):
         p = step * GROUP + i
         tile = target[p]
         shift0 = col[p] - 3
@@ -140,7 +143,7 @@
             inside = (place >= 0) & (place < half)
             above = (shift > 0).astype(jnp.float32)
             below = (shift < 0).astype(jnp.float32)
-            lines = pl.ds(pl.multiple_of(i * 64 + b * 8, 8), 8)
+            lines = slice(i * 64 + b * 8, i * 64 + b * 8 + 8)
             for z in range(2):
                 left = pltpu.roll(mixed[lines, z * width : z * width + half], turn, 1)
                 right = pltpu.roll(mixed[lines, z * width + half : (z + 1) * width], turn, 1)
@@ -169,9 +172,9 @@
         lines_ref[mate, plane, :] = jnp.where(
             slot_lane // 16 == slot, slot_line + row[p], lines_ref[mate, plane, :]
         )
-        return 0
-
-    lax.fori_loop(0, GROUP, after, 0, unroll=2)
+
+    for i in range(GROUP):
+        after(i)
 
 
 def resample(pieces, target, block, row, col, tables, taps, capacity):
@@ -311,8 +314,7 @@
                 ],
                 axis=0,
             ).astype(jnp.bfloat16)
-            for half in range(0, GROUP * 16, 128):
-                taps_ref[block, b * 8 : b * 8 + 16, half : half + 128] = pair
+            taps_ref[block, b * 8 : b * 8 + 16, :] = pair
 
     @pl.loop(1, n)
     def _(k):
@@ -335,7 +337,7 @@
         out_specs=[pl.BlockSpec(memory_space=pltpu.VMEM)] * 2,
         out_shape=[
             jax.ShapeDtypeStruct((n, 2, 1, width), jnp.float32),
-            jax.ShapeDtypeStruct((blocks, 64, GROUP * 16), jnp.bfloat16),
+            jax.ShapeDtypeStruct((blocks, 64, 128), jnp.bfloat16),
         ],
         scratch_shapes=[
             pltpu.VMEM((2, 1, width), jnp.float32),
@@ -381,7 +383,7 @@
 ):
     me = lax.axis_index("az")
     height = tile_hbm.shape[1]
-    rows = message_ref.shape[1]
+    rows, width = message_ref.shape[1:]
     m = n // MATES
     lines_fetch = pltpu.make_async_copy(lines_hbm, lines_ref, own_sem.at[0])
     tile_fetch = pltpu.make_async_copy(tile_hbm, tile_ref, own_sem.at[1])
@@ -469,19 +471,22 @@
     def order(j):
         return 1 + lax.rem(j + m // 2 - 1, m - 1) if m > 1 else 0
 
-    @pl.loop(0, m - 1)
-    def _(j):
-        for e in range(1, MATES):
-            data_copy(order(j), e).start()
-
     for e in range(1, MATES):
-        data_copy(0, e).start()
-
-    wanted = lax.broadcasted_iota(jnp.int32, (2 * height, rows), 0)
+        data_copy(order(0), e).start()
+
+    def as_bf16(value):
+        return value.astype(jnp.float32).astype(jnp.bfloat16)
+
+    wanted = as_bf16(lax.broadcasted_iota(jnp.int32, (height, rows), 0))
+    channel = lax.broadcasted_iota(jnp.int32, (rows, width), 0) // 8 % 2
+    is_imag = as_bf16(channel)
+    is_real = as_bf16(1 - channel)
 
     def placed(lines, data):
-        pick = (wanted == lines).astype(jnp.bfloat16)
-        return jnp.dot(pick, data, preferred_element_type=jnp.float32)
+        one = jnp.ones((), jnp.bfloat16)
+        pick = jnp.where(wanted == as_bf16(lines), one, jnp.zeros_like(one))
+        both = jnp.concatenate([data * is_real, data * is_imag], axis=1)
+        return jnp.dot(pick, both, preferred_element_type=jnp.float32)
 
     def summed(k):
         plane = lax.rem(high + k, m)
@@ -498,6 +503,10 @@
     @pl.loop(0, m - 1)
     def _(j):
         k = order(j)
+        following = jnp.where(j + 1 == m - 1, 0, order(j + 1))
+        for e in range(1, MATES):
+            data_copy(k, e).wait_send()
+            data_copy(following, e).start()
         part[k] = summed(k).astype(jnp.bfloat16)
         part_copy(k).start()
 
@@ -511,7 +520,7 @@
 
     tile_fetch.wait()
     ref_real, ref_imag = tile_ref[0], tile_ref[1]
-    got_real, got_imag = total[0:height, :], total[height : 2 * height, :]
+    got_real, got_imag = total[:, 0:width], total[:, width : 2 * width]
     out_ref[0] = ref_real * got_real + ref_imag * got_imag
     out_ref[1] = ref_imag * got_real - ref_real * got_imag
     tail[...] = out_ref[:, height - INTERSECTION : height, :]
@@ -551,10 +560,8 @@
     for e in range(1, MATES):
         lines_copy(e).wait_send()
 
-    @pl.loop(0, m)
-    def _(k):
-        for e in range(1, MATES):
-            data_copy(k, e).wait_send()
+    for e in range(1, MATES):
+        data_copy(0, e).wait_send()
 
     @pl.loop(1, m)
     def _(k):
@@ -585,9 +592,9 @@
             dma((2 + m,)),
             pltpu.VMEM((m, MATES, rows, width), jnp.bfloat16),
             pltpu.VMEM(lines.shape, jnp.int32),
-            pltpu.VMEM((m, 2 * height, width), jnp.bfloat16),
-            pltpu.VMEM((m, 2 * height, width), jnp.bfloat16),
-            pltpu.VMEM((2 * height, width), jnp.float32),
+            pltpu.VMEM((m, height, 2 * width), jnp.bfloat16),
+            pltpu.VMEM((m, height, 2 * width), jnp.bfloat16),
+            pltpu.VMEM((height, 2 * width), jnp.float32),
             pltpu.VMEM((2, INTERSECTION, width), jnp.float32),
             pltpu.VMEM((2, INTERSECTION, width), jnp.float32),
             dma((m, MATES)),

time: 74.5 us -> 67.7 us (0.909)
  Pallas kernels: 69.8 us -> 62.9 us
    pallas_call x1, Pallas kernels: 21 us -> 14.5 us  [resample(): pl.pallas_call(resample_kernel, grid_spec=pltpu.PrefetchScalarGridSpec(nu...]
where the time goes in v4:
time: 67.7 us; the launch traced here: 67.3 us
  Pallas kernels  62.9 us (93%)
  local copies, waits for them, and re-layouts  3.11 us (5%)
  between operations  1.3 us (2%)
    pallas_call x1, Pallas kernels, exchange(): pl.pallas_call(functools.partial(exchange_kernel, n), in_specs=[pl.BlockS...  38.1 us
    pallas_call x1, Pallas kernels, resample(): pl.pallas_call(resample_kernel, grid_spec=pltpu.PrefetchScalarGridSpec(nu...  14.5 us
    pallas_call x1, Pallas kernels, gather_tables(): pl.pallas_call(functools.partial(gather_kernel, n), in_specs=[pl.BlockSpe...  10.2 us
    unnamed x2, local copies, waits for them, and re-layouts  3.11 us

profile of v4, /device:TPU:12, one launch (start us, length us, event | category | flops | bytes accessed | tf_op | source)
XLA Modules:
  0.0 67.3 jit_solution(15122333199591424548)
XLA Ops:
  0.6 10.2 %gather_tables.1 = (f32[16,2,1,256]{3,2,1,0:T(1,128)}, bf16[64,64,128]{2,1,0:T(8,128)(2,1)}) custom-call(f32[1,256]{1,0:T(1,128)} %rate_ref.1, f32[1,256]{1,0:T(1,128)} %centre_ref.1, f32[8,8,64]{2,1,0:T(8,128)} %bitcast.2), custom_call_target="tpu_custom_call" | custom-call | tf_op jit(solution)/shard_map/gather_tables/pallas_call | solution.py:334
  10.9 14.5 %resample.1 = (bf16[128,2,8,256]{3,2,1,0:T(8,128)(2,1)}, bf16[16,256,256]{2,1,0:T(8,128)(2,1)}, s32[8,8,256]{2,1,0:T(8,128)}) custom-call(s32[128]{0:T(128)} %bitcast.3, s32[128]{0:T(128)} %block_ref.1, s32[128]{0:T(128)} %row_ref.1, s32[128]{0:T(128)} %col_ref.1, bf16[128,2,16,256]{3,2,1,0:T(8,128)(2,1)} %pieces_ref.1, ...), custom_call_target="tpu_custom_call" | custom-call | tf_op jit(solution)/shard_map/resample/pallas_call | solution.py:187
  26.1 38.1 %exchange.1 = (f32[2,256,256]{2,1,0:T(8,128)}, f32[1,2,256]{2,1,0:T(2,128)}) custom-call(s32[1]{0:T(128)S(6)} %copy.15.length_ref, bf16[16,256,256]{2,1,0:T(8,128)(2,1)} %get-tuple-element.13.message_ref, s32[8,8,256]{2,1,0:T(8,128)} %get-tuple-element.14.lines_hbm, f32[2,256,256]{2,1,0:T(8,128)} %tile_hbm.1), custom_call_target="tpu_custom_call" | custom-call | tf_op jit(solution)/shard_map/exchange/pallas_call | solution.py:580
  64.2 1.9 %copy.16 = f32[2,256,256]{2,1,0:T(8,128)} copy(f32[2,256,256]{2,1,0:T(8,128)} %get-tuple-element.21) | data formatting | bytes 1048576
  66.1 1.2 %copy.17 = f32[1,2,256]{2,1,0:T(2,128)} copy(f32[1,2,256]{2,1,0:T(2,128)} %get-tuple-element.22) | data formatting | bytes 4096

commit v5 on v4

--- a/solution.py
+++ b/solution.py
@@ -13,6 +13,7 @@
 GROUP = 16
 MATES = 8
 VMEM_BYTES = 63 * 1024 * 1024
+EXCHANGE_BYTES = 53 * 1024 * 1024
 MESH = pl.DeviceIdType.MESH
 
 SIN_FIT = (6.2831807136535645, -41.33925247192383, 81.40833282470703, -71.61119079589844)
@@ -43,9 +44,12 @@
     out_ref,
     message_ref,
     lines_ref,
-    deramped,
-    band,
-    mixed,
+    deramped_a,
+    band_a,
+    mixed_a,
+    deramped_b,
+    band_b,
+    mixed_b,
     used,
     target,
     block,
@@ -88,7 +92,8 @@
             pieces_copy(group).start()
 
         message_ref[...] = jnp.zeros_like(message_ref)
-        band[...] = jnp.zeros_like(band)
+        band_a[...] = jnp.zeros_like(band_a)
+        band_b[...] = jnp.zeros_like(band_b)
         lines_ref[...] = jnp.full_like(lines_ref, -1)
 
         @pl.loop(0, used.shape[0])
@@ -98,7 +103,8 @@
         for fetch in fetches:
             fetch.wait()
 
-    pieces_copy(step).wait()
+    pieces_copy(2 * step).wait()
+    pieces_copy(2 * step + 1).wait()
 
     in_iota = lax.broadcasted_iota(jnp.int32, (16, width), 0).astype(jnp.float32)
     out_iota = lax.broadcasted_iota(jnp.int32, (8, width), 0).astype(jnp.float32)
@@ -110,8 +116,8 @@
     def table_rows(tile):
         return 0.5 * table_ref[tile, 0], table_ref[tile, 1]
 
-    def before(i):
-        p = step * GROUP + i
+    def before(part, i, deramped, band):
+        p = (2 * step + part) * GROUP + i
         rate, centre = table_rows(target[p])
         u = (in_iota + (row[p].astype(jnp.float32) - (3.0 + TILE_ROWS / 2))) * (1.0 / TILE_ROWS)
         cosine, sine = unit_phasor((rate * u + centre) * u)
@@ -126,13 +132,9 @@
             band_lane == i % 8, taps, jnp.zeros_like(taps)
         )
 
-    for i in range(GROUP):
-        before(i)
-
-    mixed[...] = jnp.dot(band[...], deramped[...], preferred_element_type=jnp.float32)
-
-    def after(i):
-        p = step * GROUP + i
+
+    def after(part, i, mixed):
+        p = (2 * step + part) * GROUP + i
         tile = target[p]
         shift0 = col[p] - 3
         sums = [jnp.zeros((8, half), jnp.float32) for _ in range(4)]
@@ -161,8 +163,8 @@
         cosine, sine = unit_phasor((rate * u + centre) * u)
         out_real = real * cosine - imag * sine
         out_imag = imag * cosine + real * sine
-        out_ref[i, 0] = out_real.astype(jnp.bfloat16)
-        out_ref[i, 1] = out_imag.astype(jnp.bfloat16)
+        out_ref[part * GROUP + i, 0] = out_real.astype(jnp.bfloat16)
+        out_ref[part * GROUP + i, 1] = out_imag.astype(jnp.bfloat16)
         slot = used[tile]
         used[tile] = slot + 1
         message_ref[tile, pl.ds(pl.multiple_of(slot * 16, 16), 16), :] = jnp.concatenate(
@@ -173,8 +175,19 @@
             slot_lane // 16 == slot, slot_line + row[p], lines_ref[mate, plane, :]
         )
 
+    def mix(deramped, band, mixed):
+        mixed[...] = jnp.dot(band[...], deramped[...], preferred_element_type=jnp.float32)
+
     for i in range(GROUP):
-        after(i)
+        before(0, i, deramped_a, band_a)
+    mix(deramped_a, band_a, mixed_a)
+    for i in range(GROUP):
+        before(1, i, deramped_b, band_b)
+    mix(deramped_b, band_b, mixed_b)
+    for i in range(GROUP):
+        after(0, i, mixed_a)
+    for i in range(GROUP):
+        after(1, i, mixed_b)
 
 
 def resample(pieces, target, block, row, col, tables, taps, capacity):
@@ -188,21 +201,24 @@
         resample_kernel,
         grid_spec=pltpu.PrefetchScalarGridSpec(
             num_scalar_prefetch=0,
-            grid=(count // GROUP,),
+            grid=(count // (2 * GROUP),),
             in_specs=[
                 *[remote] * 5,
                 whole(*tables.shape),
                 remote,
             ],
             out_specs=[
-                pl.BlockSpec((GROUP, 2, 8, width), lambda g: (g, 0, 0, 0)),
+                pl.BlockSpec((2 * GROUP, 2, 8, width), lambda g: (g, 0, 0, 0)),
                 whole(tiles, rows, width),
                 whole(*line_shape),
             ],
             scratch_shapes=[
-                pltpu.VMEM((GROUP * 16, 2 * width), jnp.bfloat16),
-                pltpu.VMEM((GROUP * 64, GROUP * 16), jnp.bfloat16),
-                pltpu.VMEM((GROUP * 64, 2 * width), jnp.float32),
+                *[
+                    pltpu.VMEM((GROUP * 16, 2 * width), jnp.bfloat16),
+                    pltpu.VMEM((GROUP * 64, GROUP * 16), jnp.bfloat16),
+                    pltpu.VMEM((GROUP * 64, 2 * width), jnp.float32),
+                ]
+                * 2,
                 pltpu.SMEM((tiles,), jnp.int32),
                 *[pltpu.SMEM((count,), jnp.int32)] * 4,
                 pltpu.VMEM(pieces.shape, jnp.bfloat16),
@@ -521,13 +537,16 @@
     tile_fetch.wait()
     ref_real, ref_imag = tile_ref[0], tile_ref[1]
     got_real, got_imag = total[:, 0:width], total[:, width : 2 * width]
-    out_ref[0] = ref_real * got_real + ref_imag * got_imag
-    out_ref[1] = ref_imag * got_real - ref_real * got_imag
-    tail[...] = out_ref[:, height - INTERSECTION : height, :]
+    last = slice(height - INTERSECTION, height)
+    tail[0] = ref_real[last] * got_real[last] + ref_imag[last] * got_imag[last]
+    tail[1] = ref_imag[last] * got_real[last] - ref_real[last] * got_imag[last]
 
     @pl.when(me < n - 1)
     def _():
         tail_copy.start()
+
+    out_ref[0] = ref_real * got_real + ref_imag * got_imag
+    out_ref[1] = ref_imag * got_real - ref_real * got_imag
 
     length = length_ref[0]
     apart = lax.broadcasted_iota(
@@ -606,7 +625,7 @@
             dma((2,)),
         ],
         compiler_params=pltpu.CompilerParams(
-            collective_id=0, has_side_effects=True, vmem_limit_bytes=VMEM_BYTES
+            collective_id=0, has_side_effects=True, vmem_limit_bytes=EXCHANGE_BYTES
         ),
         name="exchange",
     )(length, message, lines, tile)

time: 67.7 us -> 65.3 us (0.965)
  Pallas kernels: 62.9 us -> 61.5 us
  local copies, waits for them, and re-layouts: 3.11 us -> 2.21 us
    unnamed x2 -> x4, local copies, waits for them, and re-layouts: 3.11 us -> 2.21 us
    pallas_call x1, Pallas kernels: 38.1 us -> 37.3 us  [exchange(): pl.pallas_call(functools.partial(exchange_kernel, n), in_specs=[pl.BlockS...]
where the time goes in v5:
time: 65.3 us; the launch traced here: 65 us
  Pallas kernels  61.5 us (94%)
  local copies, waits for them, and re-layouts  2.21 us (3%)
  between operations  1.31 us (2%)
    pallas_call x1, Pallas kernels, exchange(): pl.pallas_call(functools.partial(exchange_kernel, n), in_specs=[pl.BlockS...  37.3 us
    pallas_call x1, Pallas kernels, resample(): pl.pallas_call(resample_kernel, grid_spec=pltpu.PrefetchScalarGridSpec(nu...  13.9 us
    pallas_call x1, Pallas kernels, gather_tables(): pl.pallas_call(functools.partial(gather_kernel, n), in_specs=[pl.BlockSpe...  10.2 us
    unnamed x4, local copies, waits for them, and re-layouts  2.21 us

profile of v5, /device:TPU:12, one launch (start us, length us, event | category | flops | bytes accessed | tf_op | source)
XLA Modules:
  0.0 65.0 jit_solution(8854876029962721308)
XLA Ops:
  0.6 10.2 %gather_tables.1 = (f32[16,2,1,256]{3,2,1,0:T(1,128)}, bf16[64,64,128]{2,1,0:T(8,128)(2,1)}) custom-call(f32[1,256]{1,0:T(1,128)} %rate_ref.1, f32[1,256]{1,0:T(1,128)} %centre_ref.1, f32[8,8,64]{2,1,0:T(8,128)} %bitcast.2), custom_call_target="tpu_custom_call" | custom-call | tf_op jit(solution)/shard_map/gather_tables/pallas_call | solution.py:350
  10.9 13.9 %resample.1 = (bf16[128,2,8,256]{3,2,1,0:T(8,128)(2,1)}, bf16[16,256,256]{2,1,0:T(8,128)(2,1)}, s32[8,8,256]{2,1,0:T(8,128)}) custom-call(s32[128]{0:T(128)} %bitcast.3, s32[128]{0:T(128)} %block_ref.1, s32[128]{0:T(128)} %row_ref.1, s32[128]{0:T(128)} %col_ref.1, bf16[128,2,16,256]{3,2,1,0:T(8,128)(2,1)} %pieces_ref.1, ...), custom_call_target="tpu_custom_call" | custom-call | tf_op jit(solution)/shard_map/resample/pallas_call | solution.py:200
  25.5 0.0 copy-start
  25.5 0.8 %copy-done = s32[8,8,256]{2,1,0:T(8,128)S(1)} copy-done((s32[8,8,256]{2,1,0:T(8,128)S(1)}, s32[8,8,256]{2,1,0:T(8,128)}, u32[]{:S(2)}) %copy-start) | copy-done | bytes 65560
  26.3 37.3 %exchange.1 = (f32[2,256,256]{2,1,0:T(8,128)S(1)}, f32[1,2,256]{2,1,0:T(2,128)S(1)}) custom-call(s32[1]{0:T(128)S(6)} %copy.15.length_ref, bf16[16,256,256]{2,1,0:T(8,128)(2,1)} %get-tuple-element.13.message_ref, s32[8,8,256]{2,1,0:T(8,128)S(1)} %copy-done, f32[2,256,256]{2,1,0:T(8,128)} %tile_hbm.1), custom_call_target="tpu_custom_call" | custom-call | tf_op jit(solution)/shard_map/exchange/pallas_call | solution.py:599
  63.6 0.8 %copy.16 = f32[2,256,256]{2,1,0:T(8,128)} copy(f32[2,256,256]{2,1,0:T(8,128)S(1)} %get-tuple-element.21) | data formatting | bytes 1048576
  64.4 0.6 copy.17
Async XLA Ops:
  25.5 0.8 %copy-start = (s32[8,8,256]{2,1,0:T(8,128)S(1)}, s32[8,8,256]{2,1,0:T(8,128)}, u32[]{:S(2)}) copy-start(s32[8,8,256]{2,1,0:T(8,128)} %get-tuple-element.14.lines_hbm) | copy-start | bytes 196612

commit v6 on v5

--- a/solution.py
+++ b/solution.py
@@ -550,24 +550,24 @@
 
     length = length_ref[0]
     apart = lax.broadcasted_iota(
-        jnp.int32, (INTERSECTION, INTERSECTION), 1
-    ) - lax.broadcasted_iota(jnp.int32, (INTERSECTION, INTERSECTION), 0)
+        jnp.int32, (INTERSECTION, INTERSECTION), 0
+    ) - lax.broadcasted_iota(jnp.int32, (INTERSECTION, INTERSECTION), 1)
     shifter = (apart == INTERSECTION - length).astype(jnp.float32)
+    head = [
+        jnp.dot(
+            shifter,
+            out_ref[z, 0:INTERSECTION, :],
+            precision=lax.Precision.HIGHEST,
+            preferred_element_type=jnp.float32,
+        )
+        for z in range(2)
+    ]
 
     @pl.when(me > 0)
     def _():
         tail_copy.wait_recv()
 
-    before = [
-        jnp.dot(
-            shifter,
-            previous[z],
-            precision=lax.Precision.HIGHEST,
-            preferred_element_type=jnp.float32,
-        )
-        for z in range(2)
-    ]
-    head = [out_ref[z, 0:INTERSECTION, :] for z in range(2)]
+    before = [previous[z] for z in range(2)]
     scale = 1.0 / length.astype(jnp.float32)
     sum_ref[0, 0:1, :] = scale * jnp.sum(
         head[0] * before[0] + head[1] * before[1], axis=0, keepdims=True

time: 65.3 us -> 65.1 us (level)
  no operation moved by 1% of the time
where the time goes in v6:
time: 65.1 us; the launch traced here: 64.8 us
  Pallas kernels  61.3 us (94%)
  local copies, waits for them, and re-layouts  2.21 us (3%)
  between operations  1.31 us (2%)
    pallas_call x1, Pallas kernels, exchange(): pl.pallas_call(functools.partial(exchange_kernel, n), in_specs=[pl.BlockS...  37.2 us
    pallas_call x1, Pallas kernels, resample(): pl.pallas_call(resample_kernel, grid_spec=pltpu.PrefetchScalarGridSpec(nu...  13.9 us
    pallas_call x1, Pallas kernels, gather_tables(): pl.pallas_call(functools.partial(gather_kernel, n), in_specs=[pl.BlockSpe...  10.2 us
    unnamed x4, local copies, waits for them, and re-layouts  2.21 us

profile of v6, /device:TPU:12, one launch (start us, length us, event | category | flops | bytes accessed | tf_op | source)
XLA Modules:
  0.0 64.8 jit_solution(9721055728535736974)
XLA Ops:
  0.6 10.2 %gather_tables.1 = (f32[16,2,1,256]{3,2,1,0:T(1,128)}, bf16[64,64,128]{2,1,0:T(8,128)(2,1)}) custom-call(f32[1,256]{1,0:T(1,128)} %rate_ref.1, f32[1,256]{1,0:T(1,128)} %centre_ref.1, f32[8,8,64]{2,1,0:T(8,128)} %bitcast.2), custom_call_target="tpu_custom_call" | custom-call | tf_op jit(solution)/shard_map/gather_tables/pallas_call | solution.py:350
  10.9 13.9 %resample.1 = (bf16[128,2,8,256]{3,2,1,0:T(8,128)(2,1)}, bf16[16,256,256]{2,1,0:T(8,128)(2,1)}, s32[8,8,256]{2,1,0:T(8,128)}) custom-call(s32[128]{0:T(128)} %bitcast.3, s32[128]{0:T(128)} %block_ref.1, s32[128]{0:T(128)} %row_ref.1, s32[128]{0:T(128)} %col_ref.1, bf16[128,2,16,256]{3,2,1,0:T(8,128)(2,1)} %pieces_ref.1, ...), custom_call_target="tpu_custom_call" | custom-call | tf_op jit(solution)/shard_map/resample/pallas_call | solution.py:200
  25.5 0.0 copy-start
  25.5 0.8 %copy-done = s32[8,8,256]{2,1,0:T(8,128)S(1)} copy-done((s32[8,8,256]{2,1,0:T(8,128)S(1)}, s32[8,8,256]{2,1,0:T(8,128)}, u32[]{:S(2)}) %copy-start) | copy-done | bytes 65560
  26.3 37.2 %exchange.1 = (f32[2,256,256]{2,1,0:T(8,128)S(1)}, f32[1,2,256]{2,1,0:T(2,128)S(1)}) custom-call(s32[1]{0:T(128)S(6)} %copy.15.length_ref, bf16[16,256,256]{2,1,0:T(8,128)(2,1)} %get-tuple-element.13.message_ref, s32[8,8,256]{2,1,0:T(8,128)S(1)} %copy-done, f32[2,256,256]{2,1,0:T(8,128)} %tile_hbm.1), custom_call_target="tpu_custom_call" | custom-call | tf_op jit(solution)/shard_map/exchange/pallas_call | solution.py:599
  63.5 0.8 %copy.16 = f32[2,256,256]{2,1,0:T(8,128)} copy(f32[2,256,256]{2,1,0:T(8,128)S(1)} %get-tuple-element.21) | data formatting | bytes 1048576
  64.3 0.6 copy.17
Async XLA Ops:
  25.5 0.8 %copy-start = (s32[8,8,256]{2,1,0:T(8,128)S(1)}, s32[8,8,256]{2,1,0:T(8,128)}, u32[]{:S(2)}) copy-start(s32[8,8,256]{2,1,0:T(8,128)} %get-tuple-element.14.lines_hbm) | copy-start | bytes 196612
